TPU v7x, 32 devices: a whole 2x2x4 slice. The times are simulated.
32 devices in a mesh: seq: 8 (over y, x, core), row: 4 (over z).
Axes of the slice: x: 2, y: 2, z: 4, core: 2. Of those that a mesh axis runs over, the one named last changes fastest.
Arguments:
- tokens: bfloat16 [4, 1024, 2048], P('row', 'seq'), may hold values from -6 to 6
- cotangent: bfloat16 [4, 1024, 2048], P('row', 'seq'), may hold values from -6 to 6
- starts: int32 [4, 8], P('row'), may hold values from 0 to 1023, as said below
- gains: float32 [5120], P(('seq', 'row')), may hold values from 0.5 to 1.5
- gain_moment: float32 [5120], P(('seq', 'row')), may hold values from -40 to 40
- master_qa: float32 [2048, 1024], P(('seq', 'row')), may hold values from -0.125 to 0.125
- master_qb: float32 [1024, 4096], P(('seq', 'row')), may hold values from -0.1875 to 0.1875
- master_kv: float32 [2048, 512], P(('seq', 'row')), may hold values from -0.125 to 0.125
- master_out: float32 [4096, 2048], P(('seq', 'row')), may hold values from -1.5 to 1.5
- master_gu: float32 [2048, 11264], P(('seq', 'row')), may hold values from -0.125 to 0.125
- master_down: float32 [5632, 2048], P(('seq', 'row')), may hold values from -0.078125 to 0.078125
- left_stat: float32 [6144, 64, 64], P(('seq', 'row')), as said below
- right_stat: float32 [6144, 128, 128], P(('seq', 'row')), as said below
- left_root: float32 [6144, 64, 64], P(('seq', 'row')), as said below
- right_root: float32 [6144, 128, 128], P(('seq', 'row')), as said below
Outputs:
- output: bfloat16 [4, 1024, 2048], P('row', 'seq')
- grad_tokens: float32 [4, 1024, 2048], P('row', 'seq')
- grad_qa: float32 [2048, 1024], P(('seq', 'row'))
- grad_qb: float32 [1024, 4096], P(('seq', 'row'))
- grad_kv: float32 [2048, 512], P(('seq', 'row'))
- grad_out: float32 [4096, 2048], P(('seq', 'row'))
- grad_gu: float32 [2048, 11264], P(('seq', 'row'))
- grad_down: float32 [5632, 2048], P(('seq', 'row'))
- new_qa: float32 [2048, 1024], P(('seq', 'row'))
- new_qb: float32 [1024, 4096], P(('seq', 'row'))
- new_kv: float32 [2048, 512], P(('seq', 'row'))
- new_out: float32 [4096, 2048], P(('seq', 'row'))
- new_gu: float32 [2048, 11264], P(('seq', 'row'))
- new_down: float32 [5632, 2048], P(('seq', 'row'))
- moment_new: float32 [5120], P(('seq', 'row'))
- gains_new: float32 [5120], P(('seq', 'row'))
- left_new: float32 [6144, 64, 64], P(('seq', 'row'))
- right_new: float32 [6144, 128, 128], P(('seq', 'row'))
Inputs may be any that keep to these rules, and one draw needn't show every extreme that they name: Each row's starts begin at 0 and rise strictly; the last document of each row is its last position alone. In each row one document, which one drawn per row, begins before position 128 and ends after position 896. `left_stat`: each block is symmetric, with a positive diagonal larger than the sum of magnitudes of its row's other entries. `right_stat`: each block is symmetric, with a positive diagonal larger than the sum of magnitudes of its row's other entries. `left_root`: each block is symmetric, with a positive diagonal larger than the sum of magnitudes of its row's other entries. `right_root`: each block is symmetric, with a positive diagonal larger than the sum of magnitudes of its row's other entries.
All inputs are finite; a program needn't handle non-finite values.
Results may differ from a plain program's by a relative error of at most 0.015.
The roundings to bfloat16 on the way count: a program that leaves them out, or rounds other values in their place, can miss the bound.
Values may be sent and summed in bfloat16 or wider, within the bound.
No kernel may reach another device: no remote copies, remote signals or barrier semaphores. Data moves between devices by JAX's collectives and lax.ppermute only.
A program may use at most 704 MiB of HBM per device.

v0:
```python
import math

import jax
import jax.numpy as jnp
from jax import lax
from jax.sharding import PartitionSpec as P

D = 2048
QR = 1024
HQ = 16
HD = 256
FF = 5632
BL = 64
BC = 128


highest = lax.Precision.HIGHEST


def rms_norm(values, scaling):
    inverse = lax.rsqrt(jnp.mean(values * values, axis=-1, keepdims=True) + 1e-06)
    return values * inverse * scaling


def frequencies():
    half_dim = HD // 2
    return jnp.exp(jnp.arange(half_dim, dtype=jnp.float32) * (-2.0 * math.log(10000.0) / HD))


def rotate(values, cosine_table, sine_table):
    half_dim = values.shape[-1] // 2
    first_half = values[..., :half_dim]
    second_half = values[..., half_dim:]
    return jnp.concatenate(
        [
            first_half * cosine_table - second_half * sine_table,
            second_half * cosine_table + first_half * sine_table,
        ],
        axis=-1,
    )


def head_groups(values):
    tokens_here = values.shape[0]
    return jnp.moveaxis(values.reshape(tokens_here, HQ // 4, 4, HD), 1, 0)


def masked_scores(group_queries, keys_all, allowed):
    scores = jnp.einsum(
        "qhd,kd->hqk", group_queries, keys_all, preferred_element_type=jnp.float32
    ) * HD ** (-0.5)
    return jnp.where(allowed[None], scores, -1e30)


def attention_forward(queries, kv_whole, allowed):
    keys_all = kv_whole[:, :HD]
    values_all = kv_whole[:, HD:]
    tokens_here = queries.shape[0]

    def one_group(group_queries):
        scores = masked_scores(group_queries, keys_all, allowed)
        row_top = jnp.max(scores, axis=-1, keepdims=True)
        exponents = jnp.exp(scores - row_top)
        totals = jnp.sum(exponents, axis=-1, keepdims=True)
        softmax_rows = (exponents / totals).astype(jnp.bfloat16)
        result = jnp.einsum(
            "hqk,kd->qhd", softmax_rows, values_all, preferred_element_type=jnp.float32
        )
        return (result.astype(jnp.bfloat16), row_top + jnp.log(totals))

    outputs, log_total = lax.map(one_group, head_groups(queries))
    attended = jnp.moveaxis(outputs, 0, 1).reshape(tokens_here, HQ * HD)
    return (attended, log_total)


def attention_backward(queries, kv_whole, allowed, log_total, d_attended):
    keys_all = kv_whole[:, :HD]
    values_all = kv_whole[:, HD:]
    tokens_here = queries.shape[0]

    def one_group(carried, inputs):
        group_queries, group_grads, group_total = inputs
        scores = masked_scores(group_queries, keys_all, allowed)
        softmax_rows = jnp.exp(scores - group_total)
        d_probs = jnp.einsum(
            "qhd,kd->hqk", group_grads, values_all, preferred_element_type=jnp.float32
        )
        row_delta = jnp.sum(softmax_rows * d_probs, axis=-1, keepdims=True)
        d_scores = (softmax_rows * (d_probs - row_delta)).astype(jnp.bfloat16)
        d_keys = jnp.einsum(
            "hqk,qhd->kd", d_scores, group_queries, preferred_element_type=jnp.float32
        ) * HD ** (-0.5)
        d_values = jnp.einsum(
            "hqk,qhd->kd",
            softmax_rows.astype(jnp.bfloat16),
            group_grads,
            preferred_element_type=jnp.float32,
        )
        d_query = jnp.einsum(
            "hqk,kd->qhd", d_scores, keys_all, preferred_element_type=jnp.float32
        ) * HD ** (-0.5)
        return (carried + jnp.concatenate([d_keys, d_values], axis=1), d_query)

    zero_carry = jnp.zeros((kv_whole.shape[0], 2 * HD), jnp.float32)
    d_kv, d_query = lax.scan(
        one_group, zero_carry, (head_groups(queries), head_groups(d_attended), log_total)
    )
    return (d_kv, jnp.moveaxis(d_query, 0, 1).reshape(tokens_here, HQ, HD))


def forward_pass(token_rows, weights, allowed, cosine_table, sine_table, again):
    gain_values = weights[0].astype(jnp.float32)
    weight_qa = weights[1]
    weight_qb = weights[2]
    weight_kv = weights[3]
    weight_out = weights[4]
    weight_gu = weights[5]
    tokens_here = token_rows.shape[0]
    normed = rms_norm(token_rows, gain_values[:D]).astype(jnp.bfloat16)
    latent = jnp.dot(normed, weight_qa, preferred_element_type=jnp.float32)
    latent_norm = rms_norm(latent, gain_values[D : D + QR]).astype(jnp.bfloat16)
    query_lin = jnp.dot(latent_norm, weight_qb, preferred_element_type=jnp.float32).reshape(
        tokens_here, HQ, HD
    )
    queries = rotate(query_lin, cosine_table[:, None, :], sine_table[:, None, :]).astype(
        jnp.bfloat16
    )
    kv_lin = jnp.dot(normed, weight_kv, preferred_element_type=jnp.float32)
    kv_local = jnp.concatenate(
        [rotate(kv_lin[:, :HD], cosine_table, sine_table), kv_lin[:, HD:]], axis=1
    ).astype(jnp.bfloat16)
    if again:
        kv_whole = lax.all_gather(kv_local, "seq", axis=0, tiled=True)
    else:
        kv_whole = lax.all_gather(kv_local, "seq", axis=0, tiled=True)
    attended, log_total = attention_forward(queries, kv_whole, allowed)
    middle = token_rows + jnp.dot(attended, weight_out, preferred_element_type=jnp.float32)
    normed_mlp = rms_norm(middle, gain_values[D + QR :]).astype(jnp.bfloat16)
    gate_up = jnp.dot(normed_mlp, weight_gu, preferred_element_type=jnp.float32)
    hidden = (jax.nn.silu(gate_up[:, :FF]) * gate_up[:, FF:]).astype(jnp.bfloat16)
    return (
        normed,
        latent,
        latent_norm,
        queries,
        kv_whole,
        attended,
        log_total,
        middle,
        normed_mlp,
        gate_up,
        hidden,
    )


def flat_blocks(matrices):
    return jnp.concatenate([matrix.reshape(-1, BL, BC) for matrix in matrices], axis=0)


def split_blocks(blocks, shapes):
    result = []
    offset = 0
    for shape_pair in shapes:
        block_count = shape_pair[0] * shape_pair[1] // (BL * BC)
        result.append(blocks[offset : offset + block_count].reshape(shape_pair))
        offset = offset + block_count
    return result


def shampoo(grad_blocks, weight_blocks, left_stat, right_stat, left_root, right_root):
    left_new = 0.5 * left_stat + 0.5 * jnp.einsum(
        "bij,bkj->bik", grad_blocks, grad_blocks, precision=highest
    )
    right_new = 0.5 * right_stat + 0.5 * jnp.einsum(
        "bji,bjk->bik", grad_blocks, grad_blocks, precision=highest
    )
    direction = jnp.einsum("bij,bjk->bik", left_root, grad_blocks, precision=highest)
    direction = jnp.einsum("bij,bjk->bik", direction, right_root, precision=highest)
    weight_scale = jnp.sqrt(
        jnp.mean(weight_blocks * weight_blocks, axis=(1, 2), keepdims=True) + 1e-06
    )
    direction_scale = lax.rsqrt(jnp.mean(direction * direction, axis=(1, 2), keepdims=True) + 1e-06)
    return (weight_blocks - 0.3 * weight_scale * direction * direction_scale, left_new, right_new)


def on_device(
    tokens,
    cotangent,
    starts,
    gains,
    gain_moment,
    master_qa,
    master_qb,
    master_kv,
    master_out,
    master_gu,
    master_down,
    left_stat,
    right_stat,
    left_root,
    right_root,
):
    seq_count = lax.axis_size("seq")
    token_rows = tokens[0].astype(jnp.float32)
    tokens_here = token_rows.shape[0]
    length = tokens_here * seq_count
    seq_index = lax.axis_index("seq")
    places = jnp.arange(length, dtype=jnp.int32)
    starts_row = starts[0]
    inside = (starts_row[None, :] <= places[:, None]).astype(jnp.int32)
    document = jnp.sum(inside, axis=1) - 1
    first_local = seq_index * tokens_here
    local_index = first_local + jnp.arange(tokens_here, dtype=jnp.int32)
    local_doc = lax.dynamic_slice_in_dim(document, first_local, tokens_here, 0)
    picked = jnp.arange(starts_row.shape[0], dtype=jnp.int32)[None, :] == local_doc[:, None]
    local_place = local_index - jnp.sum(jnp.where(picked, starts_row[None, :], 0), axis=1)
    angles = local_place.astype(jnp.float32)[:, None] * frequencies()[None, :]
    cosine_table = jnp.cos(angles)
    sine_table = jnp.sin(angles)
    allowed = (local_doc[:, None] == document[None, :]) & (local_index[:, None] >= places[None, :])
    weights = (
        lax.all_gather(gains.astype(jnp.bfloat16), ("seq", "row"), axis=0, tiled=True),
        lax.all_gather(master_qa.astype(jnp.bfloat16), ("seq", "row"), axis=0, tiled=True),
        lax.all_gather(master_qb.astype(jnp.bfloat16), ("seq", "row"), axis=0, tiled=True),
        lax.all_gather(master_kv.astype(jnp.bfloat16), ("seq", "row"), axis=0, tiled=True),
        lax.all_gather(master_out.astype(jnp.bfloat16), ("seq", "row"), axis=0, tiled=True),
        lax.all_gather(master_gu.astype(jnp.bfloat16), ("seq", "row"), axis=0, tiled=True),
        lax.all_gather(master_down.astype(jnp.bfloat16), ("seq", "row"), axis=0, tiled=True),
    )
    activations = forward_pass(token_rows, weights, allowed, cosine_table, sine_table, False)
    output = activations[7] + jnp.dot(
        activations[10], weights[6], preferred_element_type=jnp.float32
    )
    weights = (
        lax.all_gather(gains.astype(jnp.bfloat16), ("seq", "row"), axis=0, tiled=True),
        lax.all_gather(master_qa.astype(jnp.bfloat16), ("seq", "row"), axis=0, tiled=True),
        lax.all_gather(master_qb.astype(jnp.bfloat16), ("seq", "row"), axis=0, tiled=True),
        lax.all_gather(master_kv.astype(jnp.bfloat16), ("seq", "row"), axis=0, tiled=True),
        lax.all_gather(master_out.astype(jnp.bfloat16), ("seq", "row"), axis=0, tiled=True),
        lax.all_gather(master_gu.astype(jnp.bfloat16), ("seq", "row"), axis=0, tiled=True),
        lax.all_gather(master_down.astype(jnp.bfloat16), ("seq", "row"), axis=0, tiled=True),
    )
    activations = forward_pass(token_rows, weights, allowed, cosine_table, sine_table, True)
    (
        normed,
        latent,
        latent_norm,
        queries,
        kv_whole,
        attended,
        log_total,
        middle,
        normed_mlp,
        gate_up,
        hidden,
    ) = activations
    gain_values = weights[0].astype(jnp.float32)
    gain_attn = gain_values[:D]
    gain_query = gain_values[D : D + QR]
    gain_mlp = gain_values[D + QR :]
    grad_rows = cotangent[0]
    grad_down = jnp.einsum("tf,td->fd", hidden, grad_rows, preferred_element_type=jnp.float32)
    d_hidden = jnp.einsum("td,fd->tf", grad_rows, weights[6], preferred_element_type=jnp.float32)
    gate_part = gate_up[:, :FF]
    up_part = gate_up[:, FF:]
    sigmoid_gate = jax.nn.sigmoid(gate_part)
    d_gate = d_hidden * up_part * sigmoid_gate * (1.0 + gate_part * (1.0 - sigmoid_gate))
    d_up = d_hidden * gate_part * sigmoid_gate
    d_gate_up = jnp.concatenate([d_gate, d_up], axis=1).astype(jnp.bfloat16)
    grad_gu = jnp.einsum("td,tf->df", normed_mlp, d_gate_up, preferred_element_type=jnp.float32)
    d_normed_mlp = jnp.einsum(
        "tf,df->td", d_gate_up, weights[5], preferred_element_type=jnp.float32
    )
    d_middle_part, d_gain_mlp = jax.vjp(rms_norm, middle, gain_mlp)[1](d_normed_mlp)
    d_middle = grad_rows.astype(jnp.float32) + d_middle_part
    mlp_sums = (
        lax.psum_scatter(grad_gu, ("seq", "row"), scatter_dimension=0, tiled=True),
        lax.psum_scatter(grad_down, ("seq", "row"), scatter_dimension=0, tiled=True),
    )
    d_branch = d_middle.astype(jnp.bfloat16)
    grad_out = jnp.einsum("te,td->ed", attended, d_branch, preferred_element_type=jnp.float32)
    d_attended = jnp.einsum(
        "td,ed->te", d_branch, weights[4], preferred_element_type=jnp.float32
    ).astype(jnp.bfloat16)
    d_kv, d_query = attention_backward(queries, kv_whole, allowed, log_total, d_attended)
    d_kv_local = lax.psum_scatter(d_kv, "seq", scatter_dimension=0, tiled=True)
    d_kv_lin = jnp.concatenate(
        [rotate(d_kv_local[:, :HD], cosine_table, -sine_table), d_kv_local[:, HD:]], axis=1
    ).astype(jnp.bfloat16)
    d_query_lin = (
        rotate(d_query, cosine_table[:, None, :], -sine_table[:, None, :])
        .reshape(tokens_here, HQ * HD)
        .astype(jnp.bfloat16)
    )
    grad_qb = jnp.einsum("tr,te->re", latent_norm, d_query_lin, preferred_element_type=jnp.float32)
    d_latent_norm = jnp.einsum(
        "te,re->tr", d_query_lin, weights[2], preferred_element_type=jnp.float32
    )
    d_latent, d_gain_query = jax.vjp(rms_norm, latent, gain_query)[1](d_latent_norm)
    d_latent = d_latent.astype(jnp.bfloat16)
    grad_qa = jnp.einsum("td,tr->dr", normed, d_latent, preferred_element_type=jnp.float32)
    grad_kv = jnp.einsum("td,tk->dk", normed, d_kv_lin, preferred_element_type=jnp.float32)
    d_normed = jnp.einsum(
        "tr,dr->td", d_latent, weights[1], preferred_element_type=jnp.float32
    ) + jnp.einsum("tk,dk->td", d_kv_lin, weights[3], preferred_element_type=jnp.float32)
    d_tokens_part, d_gain_attn = jax.vjp(rms_norm, token_rows, gain_attn)[1](d_normed)
    grad_tokens = d_middle + d_tokens_part
    gain_grad = jnp.concatenate([d_gain_attn, d_gain_query, d_gain_mlp])
    attn_sums = (
        lax.psum_scatter(grad_qa, ("seq", "row"), scatter_dimension=0, tiled=True),
        lax.psum_scatter(grad_qb, ("seq", "row"), scatter_dimension=0, tiled=True),
        lax.psum_scatter(grad_kv, ("seq", "row"), scatter_dimension=0, tiled=True),
        lax.psum_scatter(grad_out, ("seq", "row"), scatter_dimension=0, tiled=True),
        lax.psum_scatter(gain_grad, ("seq", "row"), scatter_dimension=0, tiled=True),
    )
    grads_local = (attn_sums[0], attn_sums[1], attn_sums[2], attn_sums[3], mlp_sums[0], mlp_sums[1])
    master_list = (master_qa, master_qb, master_kv, master_out, master_gu, master_down)
    new_blocks, left_new, right_new = shampoo(
        flat_blocks(grads_local),
        flat_blocks(master_list),
        left_stat,
        right_stat,
        left_root,
        right_root,
    )
    new_list = split_blocks(new_blocks, [matrix.shape for matrix in master_list])
    total_tokens = tokens_here * seq_count * lax.axis_size("row")
    moment_new = 0.9 * gain_moment + 0.1 * attn_sums[4]
    gains_new = gains - 0.4 / math.sqrt(total_tokens) * moment_new
    return (
        output[None].astype(jnp.bfloat16),
        grad_tokens[None],
        attn_sums[0],
        attn_sums[1],
        attn_sums[2],
        attn_sums[3],
        mlp_sums[0],
        mlp_sums[1],
        new_list[0],
        new_list[1],
        new_list[2],
        new_list[3],
        new_list[4],
        new_list[5],
        moment_new,
        gains_new,
        left_new,
        right_new,
    )


def solution(mesh):
    placed = (
        P("row", "seq", None),
        P("row", "seq", None),
        P("row", None),
        P(("seq", "row")),
        P(("seq", "row")),
        P(("seq", "row"), None),
        P(("seq", "row"), None),
        P(("seq", "row"), None),
        P(("seq", "row"), None),
        P(("seq", "row"), None),
        P(("seq", "row"), None),
        P(("seq", "row"), None, None),
        P(("seq", "row"), None, None),
        P(("seq", "row"), None, None),
        P(("seq", "row"), None, None),
    )
    return jax.shard_map(
        on_device,
        mesh=mesh,
        in_specs=placed,
        out_specs=(
            P("row", "seq", None),
            P("row", "seq", None),
            P(("seq", "row"), None),
            P(("seq", "row"), None),
            P(("seq", "row"), None),
            P(("seq", "row"), None),
            P(("seq", "row"), None),
            P(("seq", "row"), None),
            P(("seq", "row"), None),
            P(("seq", "row"), None),
            P(("seq", "row"), None),
            P(("seq", "row"), None),
            P(("seq", "row"), None),
            P(("seq", "row"), None),
            P(("seq", "row")),
            P(("seq", "row")),
            P(("seq", "row"), None, None),
            P(("seq", "row"), None, None),
        ),
        check_vma=False,
    )
```

profile of v0, /device:TPU:0, one launch (start us, length us, event | category | flops | bytes accessed | tf_op | source)
XLA Modules:
  0.0 5341.1 jit_solution(2717992858703049044)
XLA Ops:
  10.6 42.3 all-reduce
  55.4 15.3 all-gather.12.cloned.1.call-done
  98.8 63.5 %all-gather.8.cloned.1.call-done = bf16[2048,1024]{1,0:T(8,128)(2,1)} async-done(((bf16[64,1024]{1,0:T(8,128)(2,1)}), bf16[2048,1024]{1,0:T(8,128)(2,1)}) %all-gather.8.cloned.1.call-update) | async-done | bytes 4194320 | tf_op jit(solution)/shard_map/all_gather | solution.py:223
  165.3 76.3 %all-gather.10.cloned.1.call-done = bf16[1024,4096]{1,0:T(8,128)(2,1)} async-done(((bf16[32,4096]{1,0:T(8,128)(2,1)}), bf16[1024,4096]{1,0:T(8,128)(2,1)}) %all-gather.10.cloned.1.call-update) | async-done | bytes 8388624 | tf_op jit(solution)/shard_map/all_gather | solution.py:224
  248.9 18.9 while.38
  267.9 90.6 %all-gather.16.cloned.1.call-done = bf16[4096,2048]{1,0:T(8,128)(2,1)} async-done(((bf16[128,2048]{1,0:T(8,128)(2,1)}), bf16[4096,2048]{1,0:T(8,128)(2,1)}) %all-gather.16.cloned.1.call-update) | async-done | bytes 16777232 | tf_op jit(solution)/shard_map/all_gather | solution.py:226
  366.8 248.5 %all-gather.18.cloned.1.call-done = bf16[2048,11264]{1,0:T(8,128)(2,1)} async-done(((bf16[64,11264]{1,0:T(8,128)(2,1)}), bf16[2048,11264]{1,0:T(8,128)(2,1)}) %all-gather.18.cloned.1.call-update) | async-done | bytes 46137360 | tf_op jit(solution)/shard_map/all_gather | solution.py:227
  615.3 20.7 fusion.118
  636.0 125.5 %all-gather.20.cloned.1.call-done = bf16[5632,2048]{1,0:T(8,128)(2,1)} async-done(((bf16[176,2048]{1,0:T(8,128)(2,1)}), bf16[5632,2048]{1,0:T(8,128)(2,1)}) %all-gather.20.cloned.1.call-update) | async-done | bytes 23068688 | tf_op jit(solution)/shard_map/all_gather | solution.py:228
  775.8 22.9 multiply_reduce_fusion.2
  816.2 49.0 while.39
  868.6 39.0 reduce-scatter.8.cloned.1.call-done
  953.8 20.7 fusion.67
  976.1 33.4 fusion.65
  1039.7 18.2 while.37
  1066.2 20.5 fusion.81
  1103.1 42.6 all-reduce.1
  1148.6 102.0 %reduce-scatter.10.cloned.1.call-done = f32[64,1024]{1,0:T(8,128)} async-done(((f32[2048,1024]{1,0:T(8,128)}), f32[64,1024]{1,0:T(8,128)}) %reduce-scatter.10.cloned.1.call-update) | async-done | bytes 262160 | tf_op jit(solution)/shard_map/reduce_scatter | solution.py:310
  1252.3 363.1 %reduce-scatter.12.cloned.1.call-done = f32[32,4096]{1,0:T(8,128)} async-done(((f32[1024,4096]{1,0:T(8,128)}), f32[32,4096]{1,0:T(8,128)}) %reduce-scatter.12.cloned.1.call-update) | async-done | bytes 524304 | tf_op jit(solution)/shard_map/reduce_scatter | solution.py:311
  1618.1 710.1 %reduce-scatter.16.cloned.1.call-done = f32[128,2048]{1,0:T(8,128)} async-done(((f32[4096,2048]{1,0:T(8,128)}), f32[128,2048]{1,0:T(8,128)}) %reduce-scatter.16.cloned.1.call-update) | async-done | bytes 1048592 | tf_op jit(solution)/shard_map/reduce_scatter | solution.py:313
  2330.7 972.3 %reduce-scatter.20.cloned.1.call-done = f32[176,2048]{1,0:T(8,128)} async-done(((f32[5632,2048]{1,0:T(8,128)}), f32[176,2048]{1,0:T(8,128)}) %reduce-scatter.20.cloned.1.call-update) | async-done | bytes 1441808 | tf_op jit(solution)/shard_map/reduce_scatter | solution.py:278
  3305.4 1936.4 %reduce-scatter.18.cloned.1.call-done = f32[64,11264]{1,0:T(8,128)} async-done(((f32[2048,11264]{1,0:T(8,128)}), f32[64,11264]{1,0:T(8,128)}) %reduce-scatter.18.cloned.1.call-update) | async-done | bytes 2883600 | tf_op jit(solution)/shard_map/reduce_scatter | solution.py:277
  5285.4 16.3 add_multiply_fusion.1
  5308.4 25.9 add_multiply_fusion
  (350 shorter events, 337.0 us)
Async XLA Ops:
  7.2 66.9 %copy-start.30 = (f32[64,1024]{1,0:T(8,128)S(1)}, f32[64,1024]{1,0:T(8,128)}, u32[]{:S(2)}) copy-start(f32[64,1024]{1,0:T(8,128)} %param.26) | copy-start | bytes 786436
  7.2 63.5 %all-gather.12.cloned.1.call-start = ((), (), s32[]{:S(2)}) async-start(), calls=%async_computation.9 | async-start | bytes 2162688 | tf_op jit(solution)/shard_map/all_gather | solution.py:225
  8.8 87.7 %all-gather.14.cloned.1.call-start = ((), (), s32[]{:S(2)}) async-start(), calls=%async_computation.10 | async-start | bytes 1179648 | tf_op jit(solution)/shard_map/all_gather | solution.py:135
  55.4 869.4 %copy-start.46 = (f32[128]{0:T(128)}, f32[128]{0:T(128)S(1)}, u32[]{:S(2)}) copy-start(f32[128]{0:T(128)S(1)} %fusion.107) | copy-start | bytes 1540
  55.4 869.4 %copy-start.32 = (f32[2048]{0:T(1024)}, f32[2048]{0:T(1024)S(1)}, u32[]{:S(2)}) copy-start(f32[2048]{0:T(1024)S(1)} %get-tuple-element.383) | copy-start | bytes 24580
  74.1 88.2 %all-gather.8.cloned.1.call-start = ((), (), s32[]{:S(2)}) async-start(), calls=%async_computation.7 | async-start | bytes 4325376 | tf_op jit(solution)/shard_map/all_gather | solution.py:223
  74.8 166.8 %all-gather.10.cloned.1.call-start = ((), (), s32[]{:S(2)}) async-start(), calls=%async_computation.8 | async-start | bytes 8650752 | tf_op jit(solution)/shard_map/all_gather | solution.py:224
  76.7 281.8 %all-gather.16.cloned.1.call-start = ((), (), s32[]{:S(2)}) async-start(), calls=%async_computation.11 | async-start | bytes 17301504 | tf_op jit(solution)/shard_map/all_gather | solution.py:226
  78.8 536.4 %all-gather.18.cloned.1.call-start = ((), (), s32[]{:S(2)}) async-start(), calls=%async_computation.12 | async-start | bytes 47579136 | tf_op jit(solution)/shard_map/all_gather | solution.py:227
  80.1 82.1 %copy-start = (bf16[1,128,2048]{2,1,0:T(8,128)(2,1)S(1)}, bf16[1,128,2048]{2,1,0:T(8,128)(2,1)}, u32[]{:S(2)}) copy-start(bf16[1,128,2048]{2,1,0:T(8,128)(2,1)} %param.21) | copy-start | bytes 1572868
  80.2 681.3 %all-gather.20.cloned.1.call-start = ((), (), s32[]{:S(2)}) async-start(), calls=%async_computation.13 | async-start | bytes 23789568 | tf_op jit(solution)/shard_map/all_gather | solution.py:228
  82.6 825.0 %reduce-scatter.8.cloned.1.call-start = ((), (), s32[]{:S(2)}) async-start(), calls=%async_computation.14 | async-start | bytes 2359296 | tf_op jit(solution)/shard_map/reduce_scatter | solution.py:286
  165.3 81.0 %copy-start.11 = (f32[128,1024]{1,0:T(8,128)}, f32[128,1024]{1,0:T(8,128)S(1)}, u32[]{:S(2)}) copy-start(f32[128,1024]{1,0:T(8,128)S(1)} %get-tuple-element.388) | copy-start | bytes 1572868
  267.9 98.9 %copy-start.13 = (bf16[4,128,4,256]{1,3,2,0:T(8,128)(2,1)}, bf16[4,128,4,256]{1,3,2,0:T(8,128)(2,1)S(1)}, u32[]{:S(2)}) copy-start(bf16[4,128,4,256]{1,3,2,0:T(8,128)(2,1)S(1)} %get-tuple-element.137) | copy-start | bytes 3145732
  366.7 432.0 %copy-start.3 = (f32[128,2048]{1,0:T(8,128)}, f32[128,2048]{1,0:T(8,128)S(1)}, u32[]{:S(2)}) copy-start(f32[128,2048]{1,0:T(8,128)S(1)} %get-tuple-element.392) | copy-start | bytes 3145732
  615.3 146.2 %copy-start.25 = (bf16[1,128,2048]{2,1,0:T(8,128)(2,1)S(1)}, bf16[1,128,2048]{2,1,0:T(8,128)(2,1)}, u32[]{:S(2)}) copy-start(bf16[1,128,2048]{2,1,0:T(8,128)(2,1)} %param.22) | copy-start | bytes 1572868
  865.2 45.3 copy-start.1
  868.2 279.5 %reduce-scatter.14.cloned.1.call-start = ((), (), s32[]{:S(2)}) async-start(), calls=%async_computation.17 | async-start | bytes 4325376 | tf_op jit(solution)/shard_map/reduce_scatter | solution.py:312
  913.3 337.2 %reduce-scatter.10.cloned.1.call-start = ((), (), s32[]{:S(2)}) async-start(), calls=%async_computation.15 | async-start | bytes 8650752 | tf_op jit(solution)/shard_map/reduce_scatter | solution.py:310
  929.6 685.9 %reduce-scatter.12.cloned.1.call-start = ((), (), s32[]{:S(2)}) async-start(), calls=%async_computation.16 | async-start | bytes 17301504 | tf_op jit(solution)/shard_map/reduce_scatter | solution.py:311
  937.9 1390.3 %reduce-scatter.16.cloned.1.call-start = ((), (), s32[]{:S(2)}) async-start(), calls=%async_computation.18 | async-start | bytes 34603008 | tf_op jit(solution)/shard_map/reduce_scatter | solution.py:313
  952.8 2350.2 %reduce-scatter.20.cloned.1.call-start = ((), (), s32[]{:S(2)}) async-start(), calls=%async_computation.20 | async-start | bytes 47579136 | tf_op jit(solution)/shard_map/reduce_scatter | solution.py:278
  974.5 4267.4 %reduce-scatter.18.cloned.1.call-start = ((), (), s32[]{:S(2)}) async-start(), calls=%async_computation.19 | async-start | bytes 95158272 | tf_op jit(solution)/shard_map/reduce_scatter | solution.py:277
  1102.1 44.3 copy-start.10
  (49 other events, 356.7 us)
Sparse Core Ops, SparseCore 0:
  11.5 59.1 all-gather.11
  74.2 22.3 all-gather.13
  100.1 62.0 all-gather.7
  165.6 75.9 all-gather.9
  245.0 113.4 all-gather.15
  361.8 253.4 all-gather.17
  618.7 142.7 all-gather.19
  868.3 39.3 reduce-scatter.7
  913.4 148.1 reduce-scatter.13
  1065.1 185.4 reduce-scatter.9
  1253.5 361.8 reduce-scatter.11
  1618.3 709.8 reduce-scatter.15
  2331.2 971.7 reduce-scatter.19
  3305.8 1935.9 reduce-scatter.17
where the time goes:
time: 5350 us; the launch traced here: 5340 us
  waiting for transfers between devices  4760 us (89%)
  matrix products  349 us (7%)
  local copies, waits for them, and re-layouts  87.2 us (2%)
  blocking collectives  84.8 us (2%)
    reduce_scatter x1, waiting for transfers between devices, on_device(): lax.psum_scatter(grad_gu, ('seq', 'row'), scatter_dimension=0, tiled=True)  1940 us
    reduce_scatter x1, waiting for transfers between devices, on_device(): lax.psum_scatter(grad_down, ('seq', 'row'), scatter_dimension=0, tiled=True)  972 us
    reduce_scatter x1, waiting for transfers between devices, on_device(): lax.psum_scatter(grad_out, ('seq', 'row'), scatter_dimension=0, tiled=True)  710 us
    reduce_scatter x1, waiting for transfers between devices, on_device(): lax.psum_scatter(grad_qb, ('seq', 'row'), scatter_dimension=0, tiled=True)  363 us
    all_gather x1, waiting for transfers between devices, on_device(): lax.all_gather(master_gu.astype(jnp.bfloat16), ('seq', 'row'), axis=0, ti...  249 us
    all_gather x1, waiting for transfers between devices, on_device(): lax.all_gather(master_down.astype(jnp.bfloat16), ('seq', 'row'), axis=0,...  126 us
  transfers between devices with their start and end apart: 14, of which 13 were waited for; matrix products, arithmetic and copies ran while one was open for 5% of the time, Pallas kernels for 0%

commit v1 on v0

v1 whole, which is shorter than its diff:
```python
import functools
import math

import jax
import jax.numpy as jnp
import numpy as np
from jax import lax
from jax.experimental import pallas as pl
from jax.experimental.pallas import tpu as pltpu
from jax.sharding import PartitionSpec as P

D = 2048
QR = 1024
HQ = 16
HD = 256
FF = 5632
BL = 64
BC = 128
LANES = 128
GROUP = 8

bf16 = jnp.bfloat16
f32 = jnp.float32


def rms_norm(values, scaling):
    inverse = lax.rsqrt(jnp.mean(values * values, axis=-1, keepdims=True) + 1e-06)
    return values * inverse * scaling


def rms_back(values, scaling, grads):
    inverse = lax.rsqrt(jnp.mean(values * values, axis=-1, keepdims=True) + 1e-06)
    scaled = grads * scaling
    inner = jnp.mean(values * scaled, axis=-1, keepdims=True)
    d_values = inverse * scaled - values * (inverse * inverse * inverse * inner)
    d_scaling = jnp.sum(values * inverse * grads, axis=0)
    return d_values, d_scaling


def frequencies():
    half_dim = HD // 2
    return jnp.exp(jnp.arange(half_dim, dtype=f32) * (-2.0 * math.log(10000.0) / HD))


def rotate(values, cosine_table, sine_table):
    half_dim = values.shape[-1] // 2
    first_half = values[..., :half_dim]
    second_half = values[..., half_dim:]
    return jnp.concatenate(
        [
            first_half * cosine_table - second_half * sine_table,
            second_half * cosine_table + first_half * sine_table,
        ],
        axis=-1,
    )


def dot(left, right):
    return lax.dot_general(left, right, (((1,), (0,)), ((), ())), preferred_element_type=f32)


def dot_nt(left, right):
    return lax.dot_general(left, right, (((1,), (1,)), ((), ())), preferred_element_type=f32)


def dot_tn(left, right):
    return lax.dot_general(left, right, (((0,), (0,)), ((), ())), preferred_element_type=f32)


def after(value, *others):
    for other in others:
        entry = other[(0,) * other.ndim].astype(f32) * 0.0
        value = value + entry.astype(value.dtype)
    return value


def slot_order():
    order = np.zeros((2, 2, 2, 2), np.int32)
    for core in range(2):
        for a in range(2):
            for b in range(2):
                order[core, 0, a, b] = core + 2 * a + 4 * b
                order[core, 1, a, b] = core + 4 * a + 2 * b
    return order


class Layout:
    def __init__(self):
        self.n = lax.axis_size("seq")
        self.rows = lax.axis_size("row")
        self.outer = self.n // GROUP
        self.own = self.n * self.rows
        self.s = lax.axis_index("seq")
        self.r = lax.axis_index("row")
        self.i = self.s // self.outer
        self.u = self.s % self.outer

    def swap(self, values, bit):
        stride = self.outer << bit
        return lax.ppermute(values, "seq", [(s, s ^ stride) for s in range(self.n)])

    def swap_row(self, values, apart):
        return lax.ppermute(values, "row", [(r, r ^ apart) for r in range(self.rows)])

    def groups(self):
        return [[i * self.outer + u for i in range(GROUP)] for u in range(self.outer)]

    def outer_groups(self):
        return [[i * self.outer + u for u in range(self.outer)] for i in range(GROUP)]

    def gather(self, values, waits=()):
        t = values.shape[0] // 2
        first = values[:t]
        second = values[t:]
        first_near = self.swap(first, 2)
        second_near = self.swap(second, 1)
        first = jnp.concatenate([first, after(first_near, second_near, *waits)], axis=0)
        second = jnp.concatenate([second, after(second_near, first_near, *waits)], axis=0)
        first_far = self.swap(first, 1)
        second_far = self.swap(second, 2)
        both = jnp.concatenate(
            [first, after(first_far, second_far), second, after(second_far, first_far)], axis=0
        )
        return jnp.concatenate([both, self.swap(both, 0)], axis=0)

    def scatter(self, keep, send, waits=()):
        parts = after(keep + self.swap(send.astype(bf16), 0).astype(f32), *waits)
        q = parts.shape[0] // 4
        first_near = self.swap(parts[q : 2 * q].astype(bf16), 1)
        second_near = self.swap(parts[3 * q :].astype(bf16), 2)
        first = parts[:q] + after(first_near, second_near).astype(f32)
        second = parts[2 * q : 3 * q] + after(second_near, first_near).astype(f32)
        e = q // 2
        first = first[:e] + self.swap(first[e:].astype(bf16), 2).astype(f32)
        second = second[:e] + self.swap(second[e:].astype(bf16), 1).astype(f32)
        return jnp.concatenate([first, second], axis=0)

    def spread(self, values):
        t, c = values.shape
        stacked = values[None]
        for bit in (2, 1, 0):
            c = c // 2
            mine = (self.i >> bit) & 1
            keep = lax.dynamic_slice_in_dim(stacked, mine * c, c, stacked.ndim - 1)
            send = lax.dynamic_slice_in_dim(stacked, (1 - mine) * c, c, stacked.ndim - 1)
            stacked = jnp.concatenate([keep, self.swap(send, bit)], axis=0)
        stacked = stacked.reshape(2, 2, 2, 2, t // 2, c)
        halves = [stacked[:, :, :, 0], jnp.swapaxes(stacked[:, :, :, 1], 1, 2)]
        return jnp.stack(halves, axis=1).reshape(GROUP * t, c)

    def collect(self, values):
        t, c = values.shape
        t = t // GROUP
        stacked = values.reshape(2, 2, 2, 2, t // 2, c)
        halves = [stacked[:, 0], jnp.swapaxes(stacked[:, 1], 1, 2)]
        stacked = jnp.stack(halves, axis=3).reshape(GROUP * t, c)
        for bit in (0, 1, 2):
            rows = stacked.shape[0] // 2
            keep = stacked[:rows]
            other = self.swap(stacked[rows:], bit)
            high = ((self.i >> bit) & 1) == 1
            stacked = jnp.concatenate(
                [jnp.where(high, other, keep), jnp.where(high, keep, other)], axis=1
            )
        return stacked

    def scatter_dots(self, products, waits=()):
        def total(begin, end):
            return functools.reduce(
                jnp.add, [f(left[begin:end], right) for left, right, f in products]
            )

        half = products[0][0].shape[0] // 2
        send = total(half, 2 * half).astype(bf16)
        keep = total(0, half)
        return self.scatter(keep, send, waits)

    def own_rows(self, values):
        e = values.shape[0] // 16
        return jnp.concatenate([values[:e], values[4 * e : 5 * e]], axis=0)

    def gather_outer(self, values):
        if self.outer == 1:
            return values
        result = lax.all_gather(values, "seq", axis=0, axis_index_groups=self.outer_groups())
        return result.reshape((self.outer * self.rows,) + values.shape[1:])

    def gather_shard(self, values):
        flat = values.reshape(-1, values.shape[-1])
        flat = lax.all_gather(flat, "row", axis=0, tiled=True)
        return self.gather_outer(flat.reshape((self.rows,) + values.shape))

    def exchange(self, values):
        groups = None if self.outer == 1 else self.groups()
        return lax.all_to_all(values, "seq", 0, 0, axis_index_groups=groups)

    def sum_shard(self, values, *waits):
        if self.outer > 1:
            values = lax.psum_scatter(
                values.reshape(self.outer, -1, values.shape[-1]),
                "seq",
                scatter_dimension=0,
                axis_index_groups=self.outer_groups(),
                tiled=False,
            )
        values = lax.psum_scatter(values, "row", scatter_dimension=0, tiled=True)
        return after(values, *waits)

    def sum_all(self, values):
        for bit in range(self.n.bit_length() - 1):
            stride = 1 << bit
            values = values + lax.ppermute(values, "seq", [(s, s ^ stride) for s in range(self.n)])
        for bit in range(self.rows.bit_length() - 1):
            values = values + self.swap_row(values, 1 << bit)
        return values


def attention_forward(queries, keys_all, values_all, allowed):
    def one_head(head_queries):
        scores = dot_nt(head_queries, keys_all) * HD ** (-0.5)
        scores = jnp.where(allowed, scores, -1e30)
        row_top = jnp.max(scores, axis=-1, keepdims=True)
        exponents = jnp.exp(scores - row_top)
        totals = jnp.sum(exponents, axis=-1, keepdims=True)
        softmax_rows = (exponents / totals).astype(bf16)
        return dot(softmax_rows, values_all).astype(bf16), row_top + jnp.log(totals)

    pairs = [one_head(head_queries) for head_queries in queries]
    return [pair[0] for pair in pairs], [pair[1] for pair in pairs]


def attention_backward(queries, keys_all, values_all, allowed, log_totals, d_attended):
    d_keys = 0.0
    d_values = 0.0
    d_queries = []
    for head_queries, log_total, grads in zip(queries, log_totals, d_attended):
        scores = dot_nt(head_queries, keys_all) * HD ** (-0.5)
        softmax_rows = jnp.where(allowed, jnp.exp(jnp.where(allowed, scores - log_total, 0.0)), 0.0)
        d_probs = dot_nt(grads, values_all)
        row_delta = jnp.sum(softmax_rows * d_probs, axis=-1, keepdims=True)
        d_scores = (softmax_rows * (d_probs - row_delta)).astype(bf16)
        d_keys = d_keys + dot_tn(d_scores, head_queries) * HD ** (-0.5)
        d_values = d_values + dot_tn(softmax_rows.astype(bf16), grads)
        d_queries.append(dot(d_scores, keys_all) * HD ** (-0.5))
    return jnp.concatenate([d_keys, d_values], axis=1), d_queries


def column_chunks(parts, segments):
    width = parts[0].shape[1]
    piece = width // segments
    unit = LANES // 2
    if piece % LANES == 0:
        turned = parts
    else:
        turned = [pltpu.roll(part, unit, 1) for part in parts]
    lower = lax.broadcasted_iota(jnp.int32, (parts[0].shape[0], LANES), 1) < unit
    chunks = []
    for c in range(GROUP * width // LANES):
        found = []
        for half in range(2):
            segment, at = divmod(c * LANES + half * unit, GROUP * piece)
            member, at = divmod(at, piece)
            at = at + segment * piece
            if (at // unit) % 2 == half:
                found.append((False, member, at // LANES))
            else:
                found.append((True, member, ((at + unit) % width) // LANES))
        sides = [
            (turned if moved else parts)[member][:, k * LANES : (k + 1) * LANES]
            for moved, member, k in found
        ]
        chunks.append(sides[0] if found[0] == found[1] else jnp.where(lower, sides[0], sides[1]))
    return chunks


def shampoo_kernel(count, segments, g_ref, w_ref, lr_ref, rr_ref, ls_ref, rs_ref, *refs):
    grad_ref, new_ref, left_ref, right_ref, g_rows, w_rows = refs[-6:]
    height, width = w_ref.shape
    n = width // BC
    if segments:
        chunks = column_chunks([g_ref[i].astype(f32) for i in range(GROUP)], segments)
    else:
        chunks = [g_ref[:, c * BC : (c + 1) * BC].astype(f32) for c in range(n)]
    for c in range(n):
        columns = slice(c * BC, (c + 1) * BC)
        grad_ref[:, columns] = chunks[c]
        g_rows[pl.ds(c, height, stride=n), :] = chunks[c]
        w_rows[pl.ds(c, height, stride=n), :] = w_ref[:, columns]
    together = max(k for k in range(1, 12) if count % k == 0)

    def some_blocks(turn, carry):
        blocks = [turn * together + k for k in range(together)]
        rows = [pl.ds(pl.multiple_of(b * BL, BL), BL) for b in blocks]
        low = [g_rows[at, :].astype(bf16) for at in rows]
        step = [dot(lr_ref[b], x).astype(bf16) for b, x in zip(blocks, low)]
        left = [dot_nt(x, x) for x in low]
        step = [dot(x, rr_ref[b].astype(bf16)) for b, x in zip(blocks, step)]
        right = [dot_tn(x, x) for x in low]
        for b, x, y in zip(blocks, left, right):
            left_ref[b] = 0.5 * ls_ref[b] + 0.5 * x
            right_ref[b] = 0.5 * rs_ref[b] + 0.5 * y
        for at, x in zip(rows, step):
            weight = w_rows[at, :]
            weight_scale = jnp.sqrt(jnp.mean(weight * weight, keepdims=True) + 1e-06)
            step_scale = lax.rsqrt(jnp.mean(x * x, keepdims=True) + 1e-06)
            w_rows[at, :] = weight - (0.3 * weight_scale * step_scale) * x
        return carry

    lax.fori_loop(0, count // together, some_blocks, 0)
    for c in range(n):
        new_ref[:, c * BC : (c + 1) * BC] = w_rows[pl.ds(c, height, stride=n), :]


def shampoo(offset, grad, segments, weight, left_root, right_root, left_stat, right_stat, stats):
    m, width = weight.shape
    height = m
    for rows in (16, 32, 64):
        if m % rows == 0 and rows * width <= 16 * 11264 and (m // rows > 1 or height == m):
            height = rows
    count = height * width // (BL * BC)
    flat = pl.BlockSpec((height, width), lambda k: (k, 0))
    placed = lambda extent: pl.BlockSpec(
        (pl.Element(count), pl.Element(extent), pl.Element(extent)), lambda k: (k * count + offset, 0, 0)
    )
    if segments:
        given = pl.BlockSpec((GROUP, height, width // GROUP), lambda k: (0, k, 0))
    else:
        given = flat
    begun = [stat for stat in stats if stat is not None]
    blocks = m * width // (BL * BC)
    return pl.pallas_call(
        functools.partial(shampoo_kernel, count, segments),
        grid=(m // height,),
        in_specs=[given, flat, placed(BL), placed(BC), placed(BL), placed(BC)]
        + [pl.BlockSpec(memory_space=pltpu.MemorySpace.HBM)] * len(begun),
        out_specs=[flat, flat, placed(BL), placed(BC)],
        out_shape=[
            jax.ShapeDtypeStruct(weight.shape, f32),
            jax.ShapeDtypeStruct(weight.shape, f32),
            jax.ShapeDtypeStruct(left_stat.shape, f32),
            jax.ShapeDtypeStruct(right_stat.shape, f32),
        ],
        scratch_shapes=[pltpu.VMEM((height * width // BC, BC), f32)] * 2,
        input_output_aliases={6: 2, 7: 3} if begun else {},
        compiler_params=pltpu.CompilerParams(vmem_limit_bytes=48 * 1024 * 1024),
        cost_estimate=pl.CostEstimate(
            flops=blocks * 8 * BL * BC * BC,
            bytes_accessed=blocks * 4 * (3 * BC * BC + 3 * BL * BC + 3 * BL * BL),
            transcendentals=0,
        ),
        name="shampoo",
    )(grad, weight, left_root, right_root, left_stat, right_stat, *begun)


def on_device(
    tokens,
    cotangent,
    starts,
    gains,
    gain_moment,
    master_qa,
    master_qb,
    master_kv,
    master_out,
    master_gu,
    master_down,
    left_stat,
    right_stat,
    left_root,
    right_root,
):
    lay = Layout()
    tokens_here = tokens.shape[1]
    copies = lay.outer * lay.rows
    heads_here = HQ // GROUP
    hidden_here = FF // GROUP

    gains_here = gains.shape[0]
    def columns(matrix):
        m, width = matrix.shape
        return jnp.moveaxis(matrix.astype(bf16).reshape(m, GROUP, width // GROUP), 1, 0)

    def whole_shard(shard):
        return jnp.moveaxis(shard, 0, 1).reshape(-1, shard.shape[-1])

    query_parts = columns(master_qb)
    query_rows, query_width = query_parts.shape[1:]
    gain_row = jnp.pad(gains.astype(bf16), (0, query_width - gains_here))
    gain_row = jnp.broadcast_to(gain_row[None, None, :], (GROUP, 1, query_width))
    query_parts = lay.exchange(jnp.concatenate([query_parts, gain_row], axis=1))
    gain_group = query_parts[:, query_rows, :gains_here].reshape(1, -1)
    query_parts = query_parts[:, :query_rows]
    small_rows = master_qa.shape[0]
    small_width = QR + 2 * HD
    gain_group = jnp.pad(gain_group, ((0, 15), (0, small_width - gain_group.shape[1])))
    weight_small = jnp.concatenate([master_qa, master_kv], axis=1).astype(bf16)
    weight_small = lay.gather_shard(jnp.concatenate([weight_small, gain_group], axis=0))
    gain_values = weight_small[:, small_rows, : GROUP * gains_here]
    gain_values = jnp.moveaxis(gain_values.reshape(copies, GROUP, gains_here), 0, 1)
    gain_values = gain_values.reshape(-1).astype(f32)
    gain_attn = gain_values[:D]
    gain_query = gain_values[D : D + QR]
    gain_mlp = gain_values[D + QR :]
    weight_small = weight_small[:, :small_rows].reshape(-1, small_width)
    gate_up_parts = jnp.concatenate([columns(master_gu[:, :FF]), columns(master_gu[:, FF:])], axis=2)
    gate_up_parts = lay.exchange(after(gate_up_parts, query_parts))
    out_rows = master_out.shape[0]
    query_out = jnp.concatenate([query_parts.reshape(-1, D), master_out.astype(bf16)], axis=0)
    query_out = lay.gather_shard(after(query_out, weight_small))
    weight_out = query_out[:, -out_rows:].reshape(-1, D)
    split = gate_up_parts.shape[1] // 2
    gate_up_first = lay.gather_shard(after(gate_up_parts[:, :split], query_out))
    gate_up_second = lay.gather_shard(after(gate_up_parts[:, split:], gate_up_first))
    weight_gu = whole_shard(jnp.concatenate([gate_up_first, gate_up_second], axis=2))
    weight_qb = whole_shard(query_out[:, :-out_rows].reshape((copies,) + query_parts.shape))
    weight_down = lay.gather_shard(after(master_down.astype(bf16), gate_up_second)).reshape(-1, D)

    master_list = (master_qa, master_qb, master_kv, master_out, master_gu, master_down)
    left_root_low = lax.optimization_barrier(left_root.astype(bf16))
    left_stat_rows = lax.optimization_barrier(left_stat)

    half = tokens_here // 2
    order = slot_order()
    halves = np.broadcast_to(np.arange(2, dtype=np.int32)[None, :, None, None], order.shape)
    in_group = (
        (lay.i ^ jnp.asarray(order.reshape(-1, 1))) * (lay.outer * tokens_here)
        + jnp.asarray(halves.reshape(-1, 1)) * half
        + jnp.arange(half, dtype=jnp.int32)[None, :]
    ).reshape(-1)
    positions = in_group + lay.u * tokens_here
    key_positions = (
        jnp.arange(lay.outer, dtype=jnp.int32)[:, None] * tokens_here + in_group[None, :]
    ).reshape(-1)
    starts_row = starts[0]

    def document_of(places):
        return jnp.sum((starts_row[None, :] <= places[:, None]).astype(jnp.int32), axis=1) - 1

    document = document_of(positions)
    picked = jnp.arange(starts_row.shape[0], dtype=jnp.int32)[None, :] == document[:, None]
    place = positions - jnp.sum(jnp.where(picked, starts_row[None, :], 0), axis=1)
    angles = place.astype(f32)[:, None] * frequencies()[None, :]
    cosine_table = jnp.cos(angles)
    sine_table = jnp.sin(angles)
    allowed = (document[:, None] == document_of(key_positions)[None, :]) & (
        positions[:, None] >= key_positions[None, :]
    )

    token_rows = tokens[0].astype(f32)
    own_cosine = lay.own_rows(cosine_table)
    own_sine = lay.own_rows(sine_table)
    normed = rms_norm(token_rows, gain_attn).astype(bf16)
    normed_part = lay.spread(after(normed, gate_up_parts))
    latent_kv = lay.scatter_dots(
        [(normed_part, weight_small, dot)], (query_out,)
    )
    latent = latent_kv[:, :QR]
    own_keys = rotate(latent_kv[:, QR : QR + HD], own_cosine, own_sine)
    own_low = jnp.concatenate(
        [rms_norm(latent, gain_query), own_keys, latent_kv[:, QR + HD :]], axis=1
    )
    all_low = lay.gather(own_low.astype(bf16), (gate_up_first,))
    latent_norm = all_low[:, :QR]
    keys_all = all_low[:, QR : QR + HD]
    values_all = all_low[:, QR + HD :]
    query_lin = after(dot(latent_norm, weight_qb), gate_up_second)
    queries = [
        rotate(query_lin[:, h * HD : (h + 1) * HD], cosine_table, sine_table).astype(bf16)
        for h in range(heads_here)
    ]
    if lay.outer > 1:
        kv_all = lax.all_gather(
            jnp.concatenate([keys_all, values_all], axis=1),
            "seq",
            axis=0,
            tiled=True,
            axis_index_groups=lay.outer_groups(),
        )
        keys_all = kv_all[:, :HD]
        values_all = kv_all[:, HD:]
    attended, log_totals = attention_forward(queries, keys_all, values_all, allowed)
    attended = jnp.concatenate(attended, axis=1)
    middle = token_rows + lay.scatter_dots([(attended, weight_out, dot)], (weight_down,))
    normed_mlp = lay.gather(rms_norm(middle, gain_mlp).astype(bf16))
    grad_rows = lay.gather(after(cotangent[0], all_low))
    gate_up = dot(normed_mlp, weight_gu)
    gate = gate_up[:, :hidden_here]
    up = gate_up[:, hidden_here:]
    sigmoid_gate = jax.nn.sigmoid(gate)
    hidden = (gate * sigmoid_gate * up).astype(bf16)

    def column_parts(grad):
        m = grad.shape[0] // (GROUP * copies)
        parts = jnp.moveaxis(grad.reshape(GROUP, copies, m, -1), 1, 0)
        return parts.reshape(-1, grad.shape[1])

    part_down = dot_tn(hidden, grad_rows).astype(bf16)
    d_hidden = dot_nt(grad_rows, weight_down)
    d_gate = d_hidden * up * sigmoid_gate * (1.0 + gate * (1.0 - sigmoid_gate))
    d_up = d_hidden * gate * sigmoid_gate
    d_gate_up = jnp.concatenate([d_gate.astype(bf16), d_up.astype(bf16)], axis=1)
    d_gate_up = after(d_gate_up, part_down)
    part_gu = column_parts(dot_tn(normed_mlp, d_gate_up).astype(bf16))
    sum_down = lay.sum_shard(part_down)
    d_normed_mlp = lay.scatter_dots([(d_gate_up, weight_gu, dot_nt)], (part_gu,))
    d_middle_part, d_gain_mlp = rms_back(middle, gain_mlp, d_normed_mlp)
    sum_gu = lay.sum_shard(part_gu)
    d_middle = cotangent[0].astype(f32) + d_middle_part
    d_branch = lay.gather(d_middle.astype(bf16), (sum_down,))
    sizes = [matrix.size // (BL * BC) for matrix in master_list]
    offsets = [sum(sizes[:k]) for k in range(len(sizes))]
    grad_list = [None] * 6
    new_list = [None] * 6
    stats = (None, None)

    def update(k, grad, segments, stats):
        grad_list[k], new_list[k], *stats = shampoo(
            offsets[k],
            grad,
            segments,
            master_list[k],
            left_root_low,
            right_root,
            left_stat_rows,
            right_stat,
            stats,
        )
        return stats

    stats = update(5, sum_down, 0, stats)
    output = middle + lay.scatter_dots([(after(hidden, d_branch), weight_down, dot)])
    d_attended = after(dot_nt(d_branch, weight_out), new_list[5]).astype(bf16)
    d_heads = [d_attended[:, h * HD : (h + 1) * HD] for h in range(heads_here)]
    d_kv, d_queries = attention_backward(
        queries, keys_all, values_all, allowed, log_totals, d_heads
    )
    if lay.outer > 1:
        d_kv = lax.psum_scatter(
            d_kv.reshape(lay.outer, -1, 2 * HD),
            "seq",
            scatter_dimension=0,
            axis_index_groups=lay.outer_groups(),
            tiled=False,
        )
    d_query_lin = jnp.concatenate(
        [rotate(d_query, cosine_table, -sine_table).astype(bf16) for d_query in d_queries], axis=1
    )
    rows = d_query_lin.shape[0] // 2
    send = jnp.concatenate([dot_nt(d_query_lin[rows:], weight_qb), d_kv[rows:]], axis=1)
    keep = jnp.concatenate([dot_nt(d_query_lin[:rows], weight_qb), d_kv[:rows]], axis=1)
    part_qb = column_parts(dot_tn(latent_norm, d_query_lin).astype(bf16)).reshape(copies, -1, D)
    part_out = dot_tn(attended, d_branch).astype(bf16).reshape(copies, -1, D)
    part_qb_out = jnp.concatenate([part_qb, part_out], axis=1).reshape(-1, D)
    sums = lay.scatter(keep, after(send, sum_gu, output), (part_qb_out,))
    d_latent, d_gain_query = rms_back(latent, gain_query, sums[:, :QR])
    d_keys = rotate(sums[:, QR : QR + HD], own_cosine, -own_sine)
    d_low = jnp.concatenate([d_latent, d_keys, sums[:, QR + HD :]], axis=1).astype(bf16)
    sum_qb_out = lay.sum_shard(part_qb_out)
    d_low_all = lay.gather(d_low, (sum_qb_out,))
    part_small = dot_tn(normed_part, d_low_all).astype(bf16)
    d_normed = lay.collect(dot_nt(d_low_all, weight_small).astype(bf16)).astype(f32)
    d_tokens_part, d_gain_attn = rms_back(token_rows, gain_attn, d_normed)
    grad_tokens = d_middle + d_tokens_part

    gain_grad = jnp.concatenate([d_gain_attn, d_gain_query, d_gain_mlp]).reshape(-1, LANES)
    gain_grad = lay.sum_all(gain_grad).reshape(-1)
    owner = lay.s * lay.rows + lay.r
    gain_grad = lax.dynamic_slice_in_dim(gain_grad, owner * gains_here, gains_here, 0)

    sum_small = lay.sum_shard(part_small)
    sum_qb = sum_qb_out[:-out_rows].reshape(GROUP, -1, HQ * HD // GROUP)
    parts_qb = lay.exchange(after(sum_qb, part_small))
    parts_gu = lay.exchange(after(sum_gu, part_small).reshape(GROUP, -1, sum_gu.shape[1]))
    stats = update(3, sum_qb_out[-out_rows:], 0, stats)
    stats = update(4, parts_gu, 2, stats)
    stats = update(1, parts_qb, 1, stats)
    stats = update(0, sum_small[:, :QR], 0, stats)
    left_new, right_new = update(2, sum_small[:, QR:], 0, stats)
    total_tokens = tokens_here * lay.own
    moment_new = 0.9 * gain_moment + 0.1 * gain_grad
    gains_new = gains - 0.4 / math.sqrt(total_tokens) * moment_new
    return (
        output[None].astype(bf16),
        grad_tokens[None],
        *grad_list,
        *new_list,
        moment_new,
        gains_new,
        left_new,
        right_new,
    )


def solution(mesh):
    owned = P(("seq", "row"), None)
    owned_blocks = P(("seq", "row"), None, None)
    placed = (P("row", "seq", None),) * 2
    vector = P(("seq", "row"))
    return jax.shard_map(
        on_device,
        mesh=mesh,
        in_specs=placed + (P("row", None), vector, vector) + (owned,) * 6 + (owned_blocks,) * 4,
        out_specs=placed + (owned,) * 12 + (vector, vector) + (owned_blocks,) * 2,
        check_vma=False,
    )
```

time: 5350 us -> 820 us (0.15)
  waiting for transfers between devices: 4760 us -> 281 us
  matrix products: 349 us -> 94.4 us
  starting transfers between devices: 1.16 us -> 96.6 us
  blocking collectives: 84.8 us -> 22.1 us
    reduce_scatter x7 -> x4, waiting for transfers between devices: 4120 us -> 19.6 us  [sum_shard(): values = lax.psum_scatter(values, 'row', scatter_dimension=0, tiled=True)]
    all_gather x7 -> x4, waiting for transfers between devices: 634 us -> 91 us  [gather_shard(): flat = lax.all_gather(flat, 'row', axis=0, tiled=True)]
    dot_general x60 -> x32, matrix products: 349 us -> 94.4 us  [the longest x11 34.4 us: dot_nt(): lax.dot_general(left, right, (((1,), (1,)), ((), ())), preferred_element_...]
    ppermute x0 -> x61, waiting for transfers between devices: none -> 150 us  [the longest x56 140 us: swap(): return lax.ppermute(values, 'seq', [(s, s ^ stride) for s in range(self.n)])]
    unnamed x2 -> x0, blocking collectives: 84.8 us -> none
    ppermute x0 -> x61, starting transfers between devices: none -> 65 us  [the longest x56 57.7 us: swap(): return lax.ppermute(values, 'seq', [(s, s ^ stride) for s in range(self.n)])]
  transfers between devices with their start and end apart: 14 -> 73, of which waited for: 13 -> 43; matrix products, arithmetic and copies ran while one was open for 5% -> 27% of each run, Pallas kernels for 0% -> 4%
where the time goes in v1:
time: 820 us; the launch traced here: 809 us
  waiting for transfers between devices  281 us (34%)
  local copies, waits for them, and re-layouts  130 us (16%)
  starting transfers between devices  96.6 us (12%)
  matrix products  94.4 us (12%)
  other arithmetic  93.7 us (11%)
  between operations  50.2 us (6%)
  Pallas kernels  40.8 us (5%)
  blocking collectives  22.1 us (3%)
    ppermute x56, waiting for transfers between devices, swap(): return lax.ppermute(values, 'seq', [(s, s ^ stride) for s in range(self.n)])  140 us
    all_gather x4, waiting for transfers between devices, gather_shard(): flat = lax.all_gather(flat, 'row', axis=0, tiled=True)  91 us
    ppermute x56, starting transfers between devices, swap(): return lax.ppermute(values, 'seq', [(s, s ^ stride) for s in range(self.n)])  57.7 us
    unnamed x321, local copies, waits for them, and re-layouts  44.2 us
    pallas_call x6, Pallas kernels, shampoo(): pl.pallas_call(functools.partial(shampoo_kernel, count, segments), grid=(...  40.8 us
    slice x49, local copies, waits for them, and re-layouts, after(): entry = other[(0,) * other.ndim].astype(f32) * 0.0  37.3 us
    dot_general x11, matrix products, dot_nt(): lax.dot_general(left, right, (((1,), (1,)), ((), ())), preferred_element_...  34.4 us
    dot_general x12, matrix products, dot(): lax.dot_general(left, right, (((1,), (0,)), ((), ())), preferred_element_...  33.8 us
  transfers between devices with their start and end apart: 73, of which 43 were waited for; matrix products, arithmetic and copies ran while one was open for 27% of the time, Pallas kernels for 4%

profile of v1, /device:TPU:0, one launch (start us, length us, event | category | flops | bytes accessed | tf_op | source)
XLA Modules:
  0.0 808.8 jit_solution(9518036576338540777)
XLA Ops:
  24.0 22.1 %all_gather.15 = bf16[320,1536]{1,0:T(8,128)(2,1)S(1)} all-gather(bf16[80,1536]{1,0:T(8,128)(2,1)S(1)} %fusion.132), channel_id=1, replica_groups=mesh['seq'=8,'row'=4] {'row'}, dimensions={0}, use_global_device_ids=true | all-gather | bytes 1228800 | tf_op jit(solution)/shard_map/all_gather | solution.py:190
  57.6 15.4 %all-to-all-done.1 = bf16[8,64,1408]{2,1,0:T(8,128)(2,1)S(1)} async-done(((bf16[8,64,1408]{2,1,0:T(8,128)(2,1)}), bf16[8,64,1408]{2,1,0:T(8,128)(2,1)S(1)}, u32[]{:S(2)}, u32[]{:S(2)}) %all-to-all-start.1) | async-done | bytes 1441824 | tf_op jit(solution)/shard_map/all_to_all | solution.py:195
  99.8 19.4 %all-gather.5.cloned.1.call-done = bf16[768,2048]{1,0:T(8,128)(2,1)} async-done(((bf16[192,2048]{1,0:T(8,128)(2,1)}), bf16[768,2048]{1,0:T(8,128)(2,1)}) %all-gather.5.cloned.1.call-update) | async-done | bytes 3145744 | tf_op jit(solution)/shard_map/all_gather | solution.py:190
  155.7 24.2 %all-gather.7.cloned.1.call-done = bf16[1024,1408]{1,0:T(8,128)(2,1)} async-done(((bf16[256,1408]{1,0:T(8,128)(2,1)}), bf16[1024,1408]{1,0:T(8,128)(2,1)}) %all-gather.7.cloned.1.call-update) | async-done | bytes 2883600 | tf_op jit(solution)/shard_map/all_gather | solution.py:190
  189.0 7.2 collective-permute-done.11
  213.9 31.2 %all-gather.9.cloned.1.call-done = bf16[1024,1408]{1,0:T(8,128)(2,1)} async-done(((bf16[256,1408]{1,0:T(8,128)(2,1)}), bf16[1024,1408]{1,0:T(8,128)(2,1)}) %all-gather.9.cloned.1.call-update) | async-done | bytes 2883600 | tf_op jit(solution)/shard_map/all_gather | solution.py:190
  248.0 11.8 %reduce-scatter.5.cloned.1.call-start = ((), (), s32[]{:S(2)}) async-start(), calls=%async_computation.12 | async-start | bytes 3604480 | tf_op jit(solution)/shard_map/reduce_scatter | solution.py:206
  289.8 16.2 %all-gather.11.cloned.1.call-done = bf16[704,2048]{1,0:T(8,128)(2,1)} async-done(((bf16[176,2048]{1,0:T(8,128)(2,1)}), bf16[704,2048]{1,0:T(8,128)(2,1)}) %all-gather.11.cloned.1.call-update) | async-done | bytes 2883600 | tf_op jit(solution)/shard_map/all_gather | solution.py:190
  318.0 8.6 %collective-permute-done.14 = bf16[128,2048]{1,0:T(8,128)(2,1)S(1)} collective-permute-done((bf16[128,2048]{1,0:T(8,128)(2,1)S(1)}, bf16[128,2048]{1,0:T(8,128)(2,1)S(1)}, u32[]{:S(2)}, u32[]{:S(2)}) %collective-permute-start.14) | collective-permute-done | bytes 524320 | tf_op jit(solution)/shard_map/ppermute | solution.py:100
  330.9 7.0 collective-permute-done.25
  382.5 7.1 fusion.181
  389.6 8.2 %multiply_convert_fusion.3 = (bf16[1024,704]{1,0:T(8,128)(2,1)}, bf16[1024,704]{1,0:T(8,128)(2,1)}, bf16[1024,704]{1,0:T(8,128)(2,1)S(1)}) fusion(f32[1024,1408]{1,0:T(8,128)S(1)} %fusion.181, bf16[1024,2048]{1,0:T(8,128)(2,1)} %constant_dynamic-update-slice_fusion.22, bf16[704,2048]{1,0:T(8,128)(2,1)S(1)} %copy-done.53), kind=kOutput, calls=%fused_computation.30 | convolution fusion | flops 2964324352 | bytes 17170432 | tf_op jit(solution)/shard_map/dot_general | solution.py:63
  399.0 7.0 convolution_convert_fusion.1
  416.3 7.1 convolution_convert_fusion
  428.2 7.1 fusion.178
  438.3 11.6 %collective-permute-done.29 = bf16[128,2048]{1,0:T(8,128)(2,1)S(1)} collective-permute-done((bf16[128,2048]{1,0:T(8,128)(2,1)S(1)}, bf16[128,2048]{1,0:T(8,128)(2,1)S(1)}, u32[]{:S(2)}, u32[]{:S(2)}) %collective-permute-start.29) | collective-permute-done | bytes 524320 | tf_op jit(solution)/shard_map/ppermute | solution.py:100
  512.7 7.5 copy.241.ls_ref
  537.3 11.4 %shampoo.6 = (f32[176,2048]{1,0:T(8,128)}, f32[176,2048]{1,0:T(8,128)}, f32[192,64,64]{2,1,0:T(8,128)}, f32[192,128,128]{2,1,0:T(8,128)}) custom-call(bf16[176,2048]{1,0:T(8,128)(2,1)S(1)} %copy-done.15, f32[176,2048]{1,0:T(8,128)S(1)} %copy-done.5, bf16[192,64,64]{2,1,0:T(8,128)(2,1)S(1)} %copy.240.lr_ref, f32[192,128,128]{2,1,0:T(8,128)} %rr_ref.11, ...), custom_call_target="tpu_custom_call" | custom-call | flops 369098752 | bytes 15138816 | tf_op jit(solution)/shard_map/shampoo/pallas_call | solution.py:331
  612.6 9.1 %collective-permute-done.44 = bf16[128,1536]{1,0:T(8,128)(2,1)S(1)} collective-permute-done((bf16[128,1536]{1,0:T(8,128)(2,1)S(1)}, bf16[128,1536]{1,0:T(8,128)(2,1)S(1)}, u32[]{:S(2)}, u32[]{:S(2)}) %collective-permute-start.44) | collective-permute-done | bytes 393248 | tf_op jit(solution)/shard_map/ppermute | solution.py:100
  643.0 19.6 %reduce-scatter.9.cloned.1.call-done = bf16[192,2048]{1,0:T(8,128)(2,1)} async-done(((bf16[768,2048]{1,0:T(8,128)(2,1)}), bf16[192,2048]{1,0:T(8,128)(2,1)}) %reduce-scatter.9.cloned.1.call-update) | async-done | bytes 786448 | tf_op jit(solution)/shard_map/reduce_scatter | solution.py:206
  736.1 8.5 %collective-permute-done.58 = f32[40,128]{1,0:T(8,128)} collective-permute-done((f32[40,128]{1,0:T(8,128)}, f32[40,128]{1,0:T(8,128)}, u32[]{:S(2)}, u32[]{:S(2)}) %collective-permute-start.58) | collective-permute-done | bytes 20512 | tf_op jit(solution)/shard_map/ppermute | solution.py:212
  756.3 6.8 all-to-all-start.2
  767.7 13.3 %shampoo.8 = (f32[64,11264]{1,0:T(8,128)}, f32[64,11264]{1,0:T(8,128)}, f32[192,64,64]{2,1,0:T(8,128)}, f32[192,128,128]{2,1,0:T(8,128)}) custom-call(bf16[8,64,1408]{2,1,0:T(8,128)(2,1)S(1)} %copy-done.7, f32[64,11264]{1,0:T(8,128)S(1)} %copy-done.3, bf16[192,64,64]{2,1,0:T(8,128)(2,1)} %copy-done, ...), custom_call_target="tpu_custom_call", output_to_operand_aliasing={{2}: (6, {}), {3}: (7, {})} | custom-call | flops 738197504 | bytes 30277632 | tf_op jit(solution)/shard_map/shampoo/pallas_call | solution.py:331
  795.0 6.7 copy.262
  (740 shorter events, 464.7 us)
Async XLA Ops:
  49.7 23.3 %all-to-all-start.1 = ((bf16[8,64,1408]{2,1,0:T(8,128)(2,1)}), bf16[8,64,1408]{2,1,0:T(8,128)(2,1)S(1)}, u32[]{:S(2)}, u32[]{:S(2)}) async-start(bf16[8,64,1408]{2,1,0:T(8,128)(2,1)} %copy.229), calls=%async_computation.1 | async-start | bytes 2883584 | tf_op jit(solution)/shard_map/all_to_all | solution.py:195
  53.4 65.8 %all-gather.5.cloned.1.call-start = ((), (), s32[]{:S(2)}) async-start(), calls=%async_computation.8 | async-start | bytes 3932160 | tf_op jit(solution)/shard_map/all_gather | solution.py:190
  56.1 123.8 %all-gather.7.cloned.1.call-start = ((), (), s32[]{:S(2)}) async-start(), calls=%async_computation.9 | async-start | bytes 3604480 | tf_op jit(solution)/shard_map/all_gather | solution.py:190
  97.6 24.4 %collective-permute-start.3 = (bf16[512,1536]{1,0:T(8,128)(2,1)}, bf16[512,1536]{1,0:T(8,128)(2,1)}, u32[]{:S(2)}, u32[]{:S(2)}) collective-permute-start(bf16[512,1536]{1,0:T(8,128)(2,1)} %convolution_convert_fusion.5), channel_id=1, source_target_pairs={{0,4},{4,0},{8,12},{12,8},{16,20},{20,16},{24,28},{28,24},{1,5},{5... | collective-permute-start | bytes 4718600 | tf_op jit(solution)/shard_map/ppermute | solution.py:100
  122.0 123.2 %all-gather.9.cloned.1.call-start = ((), (), s32[]{:S(2)}) async-start(), calls=%async_computation.10 | async-start | bytes 3604480 | tf_op jit(solution)/shard_map/all_gather | solution.py:190
  188.9 117.0 %all-gather.11.cloned.1.call-start = ((), (), s32[]{:S(2)}) async-start(), calls=%async_computation.11 | async-start | bytes 3604480 | tf_op jit(solution)/shard_map/all_gather | solution.py:190
  248.0 231.7 %reduce-scatter.5.cloned.1.call-start = ((), (), s32[]{:S(2)}) async-start(), calls=%async_computation.12 | async-start | bytes 3604480 | tf_op jit(solution)/shard_map/reduce_scatter | solution.py:206
  276.2 31.6 %collective-permute-start.13 = (bf16[512,2048]{1,0:T(8,128)(2,1)}, bf16[512,2048]{1,0:T(8,128)(2,1)}, u32[]{:S(2)}, u32[]{:S(2)}) collective-permute-start(bf16[512,2048]{1,0:T(8,128)(2,1)} %convolution_convert_fusion.4), channel_id=1, source_target_pairs={{0,4},{4,0},{8,12},{12,8},{16,20},{20,16},{24,28},{28,24},{1,5},{5... | collective-permute-start | bytes 6291464 | tf_op jit(solution)/shard_map/ppermute | solution.py:100
  288.3 27.9 %collective-permute-start.26 = (bf16[128,2048]{1,0:T(8,128)(2,1)}, bf16[128,2048]{1,0:T(8,128)(2,1)}, u32[]{:S(2)}, u32[]{:S(2)}) collective-permute-start(bf16[128,2048]{1,0:T(8,128)(2,1)} %pad_maximum_fusion.14), channel_id=1, source_target_pairs={{0,16},{4,20},{8,24},{12,28},{16,0},{20,4},{24,8},{28,12},{1,17},{... | collective-permute-start | bytes 1572872 | tf_op jit(solution)/shard_map/ppermute | solution.py:100
  311.8 14.9 %collective-permute-start.14 = (bf16[128,2048]{1,0:T(8,128)(2,1)S(1)}, bf16[128,2048]{1,0:T(8,128)(2,1)S(1)}, u32[]{:S(2)}, u32[]{:S(2)}) collective-permute-start(bf16[128,2048]{1,0:T(8,128)(2,1)S(1)} %get-tuple-element.245), channel_id=1, source_target_pairs={{0,8},{4,12},{8,0},{12,4},{16,24},{20,28},{24,16},{28,20},{1,9},{5... | collective-permute-start | bytes 1572872 | tf_op jit(solution)/shard_map/ppermute | solution.py:100
  313.3 14.5 %collective-permute-start.15 = (bf16[128,2048]{1,0:T(8,128)(2,1)S(1)}, bf16[128,2048]{1,0:T(8,128)(2,1)S(1)}, u32[]{:S(2)}, u32[]{:S(2)}) collective-permute-start(bf16[128,2048]{1,0:T(8,128)(2,1)S(1)} %get-tuple-element.246), channel_id=1, source_target_pairs={{0,16},{4,20},{8,24},{12,28},{16,0},{20,4},{24,8},{28,12},{1,17},{... | collective-permute-start | bytes 1572872 | tf_op jit(solution)/shard_map/ppermute | solution.py:100
  314.9 23.0 %collective-permute-start.25 = (bf16[128,2048]{1,0:T(8,128)(2,1)S(1)}, bf16[128,2048]{1,0:T(8,128)(2,1)S(1)}, u32[]{:S(2)}, u32[]{:S(2)}) collective-permute-start(bf16[128,2048]{1,0:T(8,128)(2,1)S(1)} %pad_maximum_fusion.13), channel_id=1, source_target_pairs={{0,8},{4,12},{8,0},{12,4},{16,24},{20,28},{24,16},{28,20},{1,9},{5... | collective-permute-start | bytes 1572872 | tf_op jit(solution)/shard_map/ppermute | solution.py:100
  407.2 181.8 %reduce-scatter.7.cloned.1.call-start = ((), (), s32[]{:S(2)}) async-start(), calls=%async_computation.13 | async-start | bytes 7208960 | tf_op jit(solution)/shard_map/reduce_scatter | solution.py:206
  435.5 14.4 %collective-permute-start.29 = (bf16[128,2048]{1,0:T(8,128)(2,1)S(1)}, bf16[128,2048]{1,0:T(8,128)(2,1)S(1)}, u32[]{:S(2)}, u32[]{:S(2)}) collective-permute-start(bf16[128,2048]{1,0:T(8,128)(2,1)S(1)} %get-tuple-element.243), channel_id=1, source_target_pairs={{0,8},{4,12},{8,0},{12,4},{16,24},{20,28},{24,16},{28,20},{1,9},{5... | collective-permute-start | bytes 1572872 | tf_op jit(solution)/shard_map/ppermute | solution.py:100
  436.8 14.2 %collective-permute-start.30 = (bf16[128,2048]{1,0:T(8,128)(2,1)S(1)}, bf16[128,2048]{1,0:T(8,128)(2,1)S(1)}, u32[]{:S(2)}, u32[]{:S(2)}) collective-permute-start(bf16[128,2048]{1,0:T(8,128)(2,1)S(1)} %get-tuple-element.244), channel_id=1, source_target_pairs={{0,16},{4,20},{8,24},{12,28},{16,0},{20,4},{24,8},{28,12},{1,17},{... | collective-permute-start | bytes 1572872 | tf_op jit(solution)/shard_map/ppermute | solution.py:100
  467.8 17.1 %collective-permute-start.33 = (bf16[512,2048]{1,0:T(8,128)(2,1)}, bf16[512,2048]{1,0:T(8,128)(2,1)}, u32[]{:S(2)}, u32[]{:S(2)}) collective-permute-start(bf16[512,2048]{1,0:T(8,128)(2,1)} %convolution_convert_fusion.3), channel_id=1, source_target_pairs={{0,4},{4,0},{8,12},{12,8},{16,20},{20,16},{24,28},{28,24},{1,5},{5... | collective-permute-start | bytes 6291464 | tf_op jit(solution)/shard_map/ppermute | solution.py:100
  470.8 191.9 %reduce-scatter.9.cloned.1.call-start = ((), (), s32[]{:S(2)}) async-start(), calls=%async_computation.14 | async-start | bytes 3932160 | tf_op jit(solution)/shard_map/reduce_scatter | solution.py:206
  504.2 46.6 %collective-permute-start.42 = (bf16[512,2048]{1,0:T(8,128)(2,1)}, bf16[512,2048]{1,0:T(8,128)(2,1)}, u32[]{:S(2)}, u32[]{:S(2)}) collective-permute-start(bf16[512,2048]{1,0:T(8,128)(2,1)} %get-tuple-element.273), channel_id=1, source_target_pairs={{0,4},{4,0},{8,12},{12,8},{16,20},{20,16},{24,28},{28,24},{1,5},{5... | collective-permute-start | bytes 6291464 | tf_op jit(solution)/shard_map/ppermute | solution.py:100
  505.2 14.9 %collective-permute-start.34 = (bf16[128,2048]{1,0:T(8,128)(2,1)}, bf16[128,2048]{1,0:T(8,128)(2,1)}, u32[]{:S(2)}, u32[]{:S(2)}) collective-permute-start(bf16[128,2048]{1,0:T(8,128)(2,1)} %get-tuple-element.241), channel_id=1, source_target_pairs={{0,8},{4,12},{8,0},{12,4},{16,24},{20,28},{24,16},{28,20},{1,9},{5... | collective-permute-start | bytes 1572872 | tf_op jit(solution)/shard_map/ppermute | solution.py:100
  505.9 16.0 %collective-permute-start.35 = (bf16[128,2048]{1,0:T(8,128)(2,1)}, bf16[128,2048]{1,0:T(8,128)(2,1)}, u32[]{:S(2)}, u32[]{:S(2)}) collective-permute-start(bf16[128,2048]{1,0:T(8,128)(2,1)} %get-tuple-element.242), channel_id=1, source_target_pairs={{0,16},{4,20},{8,24},{12,28},{16,0},{20,4},{24,8},{28,12},{1,17},{... | collective-permute-start | bytes 1572872 | tf_op jit(solution)/shard_map/ppermute | solution.py:100
  603.2 184.7 %reduce-scatter.11.cloned.1.call-start = ((), (), s32[]{:S(2)}) async-start(), calls=%async_computation.15 | async-start | bytes 983040 | tf_op jit(solution)/shard_map/reduce_scatter | solution.py:206
  725.7 29.6 %all-to-all-start.3 = ((bf16[8,64,1408]{2,1,0:T(8,128)(2,1)}), bf16[8,64,1408]{2,1,0:T(8,128)(2,1)S(1)}, u32[]{:S(2)}, u32[]{:S(2)}) async-start(bf16[8,64,1408]{2,1,0:T(8,128)(2,1)} %bitcast.230), calls=%async_computation.7 | async-start | bytes 2883584 | tf_op jit(solution)/shard_map/all_to_all | solution.py:195
  730.6 13.9 %collective-permute-start.58 = (f32[40,128]{1,0:T(8,128)}, f32[40,128]{1,0:T(8,128)}, u32[]{:S(2)}, u32[]{:S(2)}) collective-permute-start(f32[40,128]{1,0:T(8,128)} %fusion.214), channel_id=1, source_target_pairs={{0,16},{4,20},{8,24},{12,28},{16,0},{20,4},{24,8},{28,12},{1,17},{... | collective-permute-start | bytes 61448 | tf_op jit(solution)/shard_map/ppermute | solution.py:212
  756.3 24.6 %all-to-all-start.2 = ((bf16[8,32,512]{2,1,0:T(8,128)(2,1)}), bf16[8,32,512]{2,1,0:T(8,128)(2,1)S(1)}, u32[]{:S(2)}, u32[]{:S(2)}) async-start(bf16[8,32,512]{2,1,0:T(8,128)(2,1)} %add.779), calls=%async_computation.6 | async-start | bytes 524288 | tf_op jit(solution)/shard_map/all_to_all | solution.py:195
  (200 other events, 2332.7 us)
Sparse Core Ops, SparseCore 0:
  56.4 62.7 all-gather.4
  122.1 57.8 all-gather.6
  189.0 56.0 all-gather.8
  248.1 57.8 all-gather.10
  407.3 55.2 reduce-scatter.4
  470.9 100.3 reduce-scatter.6
  603.3 59.2 reduce-scatter.8
  721.7 22.7 reduce-scatter.10

commit v2 on v1

--- a/solution.py
+++ b/solution.py
@@ -164,14 +164,14 @@
             )
         return stacked
 
-    def scatter_dots(self, products, waits=()):
+    def scatter_dots(self, products, waits=(), send_waits=()):
         def total(begin, end):
             return functools.reduce(
                 jnp.add, [f(left[begin:end], right) for left, right, f in products]
             )
 
         half = products[0][0].shape[0] // 2
-        send = total(half, 2 * half).astype(bf16)
+        send = after(total(half, 2 * half), *send_waits).astype(bf16)
         keep = total(0, half)
         return self.scatter(keep, send, waits)
 
@@ -205,14 +205,6 @@
             )
         values = lax.psum_scatter(values, "row", scatter_dimension=0, tiled=True)
         return after(values, *waits)
-
-    def sum_all(self, values):
-        for bit in range(self.n.bit_length() - 1):
-            stride = 1 << bit
-            values = values + lax.ppermute(values, "seq", [(s, s ^ stride) for s in range(self.n)])
-        for bit in range(self.rows.bit_length() - 1):
-            values = values + self.swap_row(values, 1 << bit)
-        return values
 
 
 def attention_forward(queries, keys_all, values_all, allowed):
@@ -416,8 +408,7 @@
     weight_down = lay.gather_shard(after(master_down.astype(bf16), gate_up_second)).reshape(-1, D)
 
     master_list = (master_qa, master_qb, master_kv, master_out, master_gu, master_down)
-    left_root_low = lax.optimization_barrier(left_root.astype(bf16))
-    left_stat_rows = lax.optimization_barrier(left_stat)
+    left_root_low = left_root.astype(bf16)
 
     half = tokens_here // 2
     order = slot_order()
@@ -463,7 +454,7 @@
     latent_norm = all_low[:, :QR]
     keys_all = all_low[:, QR : QR + HD]
     values_all = all_low[:, QR + HD :]
-    query_lin = after(dot(latent_norm, weight_qb), gate_up_second)
+    query_lin = dot(latent_norm, weight_qb)
     queries = [
         rotate(query_lin[:, h * HD : (h + 1) * HD], cosine_table, sine_table).astype(bf16)
         for h in range(heads_here)
@@ -480,8 +471,8 @@
         values_all = kv_all[:, HD:]
     attended, log_totals = attention_forward(queries, keys_all, values_all, allowed)
     attended = jnp.concatenate(attended, axis=1)
-    middle = token_rows + lay.scatter_dots([(attended, weight_out, dot)], (weight_down,))
-    normed_mlp = lay.gather(rms_norm(middle, gain_mlp).astype(bf16))
+    middle = token_rows + lay.scatter_dots([(attended, weight_out, dot)], (gate_up_second,))
+    normed_mlp = lay.gather(rms_norm(middle, gain_mlp).astype(bf16), (weight_down,))
     grad_rows = lay.gather(after(cotangent[0], all_low))
     gate_up = dot(normed_mlp, weight_gu)
     gate = gate_up[:, :hidden_here]
@@ -499,10 +490,9 @@
     d_gate = d_hidden * up * sigmoid_gate * (1.0 + gate * (1.0 - sigmoid_gate))
     d_up = d_hidden * gate * sigmoid_gate
     d_gate_up = jnp.concatenate([d_gate.astype(bf16), d_up.astype(bf16)], axis=1)
-    d_gate_up = after(d_gate_up, part_down)
     part_gu = column_parts(dot_tn(normed_mlp, d_gate_up).astype(bf16))
     sum_down = lay.sum_shard(part_down)
-    d_normed_mlp = lay.scatter_dots([(d_gate_up, weight_gu, dot_nt)], (part_gu,))
+    d_normed_mlp = lay.scatter_dots([(d_gate_up, weight_gu, dot_nt)], (part_gu,), (part_down,))
     d_middle_part, d_gain_mlp = rms_back(middle, gain_mlp, d_normed_mlp)
     sum_gu = lay.sum_shard(part_gu)
     d_middle = cotangent[0].astype(f32) + d_middle_part
@@ -521,14 +511,13 @@
             master_list[k],
             left_root_low,
             right_root,
-            left_stat_rows,
+            left_stat,
             right_stat,
             stats,
         )
         return stats
 
     stats = update(5, sum_down, 0, stats)
-    output = middle + lay.scatter_dots([(after(hidden, d_branch), weight_down, dot)])
     d_attended = after(dot_nt(d_branch, weight_out), new_list[5]).astype(bf16)
     d_heads = [d_attended[:, h * HD : (h + 1) * HD] for h in range(heads_here)]
     d_kv, d_queries = attention_backward(
@@ -551,28 +540,31 @@
     part_qb = column_parts(dot_tn(latent_norm, d_query_lin).astype(bf16)).reshape(copies, -1, D)
     part_out = dot_tn(attended, d_branch).astype(bf16).reshape(copies, -1, D)
     part_qb_out = jnp.concatenate([part_qb, part_out], axis=1).reshape(-1, D)
-    sums = lay.scatter(keep, after(send, sum_gu, output), (part_qb_out,))
+    sums = lay.scatter(keep, after(send, sum_gu), (part_qb_out,))
     d_latent, d_gain_query = rms_back(latent, gain_query, sums[:, :QR])
     d_keys = rotate(sums[:, QR : QR + HD], own_cosine, -own_sine)
     d_low = jnp.concatenate([d_latent, d_keys, sums[:, QR + HD :]], axis=1).astype(bf16)
     sum_qb_out = lay.sum_shard(part_qb_out)
-    d_low_all = lay.gather(d_low, (sum_qb_out,))
+    parts_gu = lay.exchange(sum_gu.reshape(GROUP, -1, sum_gu.shape[1]))
+    stats = update(4, parts_gu, 2, stats)
+    d_low_all = lay.gather(d_low, (sum_qb_out, new_list[4]))
     part_small = dot_tn(normed_part, d_low_all).astype(bf16)
     d_normed = lay.collect(dot_nt(d_low_all, weight_small).astype(bf16)).astype(f32)
     d_tokens_part, d_gain_attn = rms_back(token_rows, gain_attn, d_normed)
     grad_tokens = d_middle + d_tokens_part
 
     gain_grad = jnp.concatenate([d_gain_attn, d_gain_query, d_gain_mlp]).reshape(-1, LANES)
-    gain_grad = lay.sum_all(gain_grad).reshape(-1)
-    owner = lay.s * lay.rows + lay.r
-    gain_grad = lax.dynamic_slice_in_dim(gain_grad, owner * gains_here, gains_here, 0)
-
+    gain_grad = jnp.pad(
+        gain_grad.reshape(lay.own, gains_here), ((0, 0), (0, -gains_here % LANES))
+    )
+    gain_grad = lax.all_to_all(gain_grad, ("seq", "row"), 0, 0, tiled=True)
+    gain_grad = jnp.sum(gain_grad, axis=0)[:gains_here]
+
+    output = middle + lay.scatter_dots([(after(hidden, part_small), weight_down, dot)])
     sum_small = lay.sum_shard(part_small)
     sum_qb = sum_qb_out[:-out_rows].reshape(GROUP, -1, HQ * HD // GROUP)
     parts_qb = lay.exchange(after(sum_qb, part_small))
-    parts_gu = lay.exchange(after(sum_gu, part_small).reshape(GROUP, -1, sum_gu.shape[1]))
     stats = update(3, sum_qb_out[-out_rows:], 0, stats)
-    stats = update(4, parts_gu, 2, stats)
     stats = update(1, parts_qb, 1, stats)
     stats = update(0, sum_small[:, :QR], 0, stats)
     left_new, right_new = update(2, sum_small[:, QR:], 0, stats)

time: 820 us -> 786 us (0.959)
  other arithmetic: 93.7 us -> 77.3 us
  starting transfers between devices: 96.6 us -> 80.8 us
    ppermute x56, waiting for transfers between devices: 140 us -> 155 us  [swap(): return lax.ppermute(values, 'seq', [(s, s ^ stride) for s in range(self.n)])]
    unnamed x321 -> x327, local copies, waits for them, and re-layouts: 44.2 us -> 56.1 us
    optimization_barrier x2 -> x0, local copies, waits for them, and re-layouts: 11.9 us -> none  [the longest x1 7.47 us: on_device(): left_stat_rows = lax.optimization_barrier(left_stat)]
    reduce_scatter x4, starting transfers between devices: 12.1 us -> 0.78 us  [sum_shard(): values = lax.psum_scatter(values, 'row', scatter_dimension=0, tiled=True)]
    all_gather x4, waiting for transfers between devices: 91 us -> 80.4 us  [gather_shard(): flat = lax.all_gather(flat, 'row', axis=0, tiled=True)]
    ppermute x5 -> x0, waiting for transfers between devices: 10.4 us -> none  [the longest x3 8.47 us: sum_all(): lax.ppermute(values, 'seq', [(s, s ^ stride) for s in range(self.n)])]
    slice x49 -> x47, local copies, waits for them, and re-layouts: 37.3 us -> 37.5 us  [after(): entry = other[(0,) * other.ndim].astype(f32) * 0.0]
  transfers between devices with their start and end apart: 73 -> 69, of which waited for: 43 -> 38; matrix products, arithmetic and copies ran while one was open for 27% -> 26% of each run, Pallas kernels for 4% -> 5%
where the time goes in v2:
time: 786 us; the launch traced here: 775 us
  waiting for transfers between devices  274 us (35%)
  local copies, waits for them, and re-layouts  131 us (17%)
  matrix products  99.6 us (13%)
  starting transfers between devices  80.8 us (10%)
  other arithmetic  77.3 us (10%)
  between operations  48.7 us (6%)
  Pallas kernels  40.7 us (5%)
  blocking collectives  22.3 us (3%)
    ppermute x56, waiting for transfers between devices, swap(): return lax.ppermute(values, 'seq', [(s, s ^ stride) for s in range(self.n)])  155 us
    all_gather x4, waiting for transfers between devices, gather_shard(): flat = lax.all_gather(flat, 'row', axis=0, tiled=True)  80.4 us
    ppermute x56, starting transfers between devices, swap(): return lax.ppermute(values, 'seq', [(s, s ^ stride) for s in range(self.n)])  58.4 us
    unnamed x327, local copies, waits for them, and re-layouts  56.1 us
    pallas_call x6, Pallas kernels, shampoo(): pl.pallas_call(functools.partial(shampoo_kernel, count, segments), grid=(...  40.7 us
    dot_general x11, matrix products, dot_nt(): lax.dot_general(left, right, (((1,), (1,)), ((), ())), preferred_element_...  37.7 us
    slice x47, local copies, waits for them, and re-layouts, after(): entry = other[(0,) * other.ndim].astype(f32) * 0.0  37.5 us
    dot_general x12, matrix products, dot(): lax.dot_general(left, right, (((1,), (0,)), ((), ())), preferred_element_...  33.3 us
  transfers between devices with their start and end apart: 69, of which 38 were waited for; matrix products, arithmetic and copies ran while one was open for 26% of the time, Pallas kernels for 5%

profile of v2, /device:TPU:0, one launch (start us, length us, event | category | flops | bytes accessed | tf_op | source)
XLA Modules:
  0.0 774.8 jit_solution(12659390871454338928)
XLA Ops:
  25.8 22.3 %all_gather.15 = bf16[320,1536]{1,0:T(8,128)(2,1)S(1)} all-gather(bf16[80,1536]{1,0:T(8,128)(2,1)S(1)} %fusion.132), channel_id=1, replica_groups=mesh['seq'=8,'row'=4] {'row'}, dimensions={0}, use_global_device_ids=true | all-gather | bytes 1228800 | tf_op jit(solution)/shard_map/all_gather | solution.py:190
  59.9 15.8 %all-to-all-done.1 = bf16[8,64,1408]{2,1,0:T(8,128)(2,1)S(1)} async-done(((bf16[8,64,1408]{2,1,0:T(8,128)(2,1)}), bf16[8,64,1408]{2,1,0:T(8,128)(2,1)S(1)}, u32[]{:S(2)}, u32[]{:S(2)}) %all-to-all-start.1) | async-done | bytes 1441824 | tf_op jit(solution)/shard_map/all_to_all | solution.py:195
  99.2 22.7 %all-gather.5.cloned.1.call-done = bf16[768,2048]{1,0:T(8,128)(2,1)} async-done(((bf16[192,2048]{1,0:T(8,128)(2,1)}), bf16[768,2048]{1,0:T(8,128)(2,1)}) %all-gather.5.cloned.1.call-update) | async-done | bytes 3145744 | tf_op jit(solution)/shard_map/all_gather | solution.py:190
  158.5 24.2 %all-gather.7.cloned.1.call-done = bf16[1024,1408]{1,0:T(8,128)(2,1)} async-done(((bf16[256,1408]{1,0:T(8,128)(2,1)}), bf16[1024,1408]{1,0:T(8,128)(2,1)}) %all-gather.7.cloned.1.call-update) | async-done | bytes 2883600 | tf_op jit(solution)/shard_map/all_gather | solution.py:190
  244.9 24.7 %all-gather.9.cloned.1.call-done = bf16[1024,1408]{1,0:T(8,128)(2,1)} async-done(((bf16[256,1408]{1,0:T(8,128)(2,1)}), bf16[1024,1408]{1,0:T(8,128)(2,1)}) %all-gather.9.cloned.1.call-update) | async-done | bytes 2883600 | tf_op jit(solution)/shard_map/all_gather | solution.py:190
  283.8 7.9 %collective-permute-done.14 = bf16[128,2048]{1,0:T(8,128)(2,1)S(1)} collective-permute-done((bf16[128,2048]{1,0:T(8,128)(2,1)S(1)}, bf16[128,2048]{1,0:T(8,128)(2,1)S(1)}, u32[]{:S(2)}, u32[]{:S(2)}) %collective-permute-start.14) | collective-permute-done | bytes 524320 | tf_op jit(solution)/shard_map/ppermute | solution.py:100
  295.9 7.1 collective-permute-done.25
  321.5 8.8 %all-gather.11.cloned.1.call-done = bf16[704,2048]{1,0:T(8,128)(2,1)} async-done(((bf16[176,2048]{1,0:T(8,128)(2,1)}), bf16[704,2048]{1,0:T(8,128)(2,1)}) %all-gather.11.cloned.1.call-update) | async-done | bytes 2883600 | tf_op jit(solution)/shard_map/all_gather | solution.py:190
  364.4 6.7 fusion.181
  371.1 8.4 %multiply_convert_fusion.2 = (bf16[1024,704]{1,0:T(8,128)(2,1)}, bf16[1024,704]{1,0:T(8,128)(2,1)}, bf16[1024,704]{1,0:T(8,128)(2,1)S(1)}) fusion(f32[1024,1408]{1,0:T(8,128)S(1)} %fusion.181, bf16[1024,2048]{1,0:T(8,128)(2,1)} %constant_dynamic-update-slice_fusion.22, bf16[704,2048]{1,0:T(8,128)(2,1)S(1)} %copy-done.47), kind=kOutput, calls=%fused_computation.34 | convolution fusion | flops 2964324352 | bytes 17170432 | tf_op jit(solution)/shard_map/dot_general | solution.py:63
  380.6 7.0 convolution_convert_fusion.1
  389.4 7.9 %add_convert_fusion = bf16[512,2048]{1,0:T(8,128)(2,1)} fusion(bf16[2048,1408]{1,0:T(8,128)(2,1)} %bitcast.229, f32[]{:T(128)} %bitcast.59, bf16[1024,704]{1,0:T(8,128)(2,1)} %get-tuple-element.205, bf16[1024,704]{1,0:T(8,128)(2,1)} %get-tuple-element.204), kind=kOutput, calls=%fused_computation.9 | convolution fusion | flops 2957770752 | bytes 10747908 | tf_op jit(solution)/shard_map/dot_general | solution.py:63
  397.4 9.7 %convolution_convert_fusion = bf16[2048,1408]{1,0:T(8,128)(2,1)S(1)} fusion(bf16[1024,2048]{1,0:T(8,128)(2,1)} %copy-done.130, bf16[1024,704]{1,0:T(8,128)(2,1)} %get-tuple-element.204, bf16[1024,704]{1,0:T(8,128)(2,1)} %get-tuple-element.205), kind=kOutput, calls=%fused_computation | convolution fusion | flops 5914230784 | bytes 12845056 | tf_op jit(solution)/shard_map/dot_general | solution.py:67
  412.0 7.2 fusion.179
  422.3 11.4 %collective-permute-done.29 = bf16[128,2048]{1,0:T(8,128)(2,1)S(1)} collective-permute-done((bf16[128,2048]{1,0:T(8,128)(2,1)S(1)}, bf16[128,2048]{1,0:T(8,128)(2,1)S(1)}, u32[]{:S(2)}, u32[]{:S(2)}) %collective-permute-start.29) | collective-permute-done | bytes 524320 | tf_op jit(solution)/shard_map/ppermute | solution.py:100
  462.7 8.4 %collective-permute-done.36 = bf16[128,2048]{1,0:T(8,128)(2,1)S(1)} collective-permute-done((bf16[128,2048]{1,0:T(8,128)(2,1)S(1)}, bf16[128,2048]{1,0:T(8,128)(2,1)S(1)}, u32[]{:S(2)}, u32[]{:S(2)}) %collective-permute-start.36) | collective-permute-done | bytes 524320 | tf_op jit(solution)/shard_map/ppermute | solution.py:100
  485.2 7.6 copy.228.ls_ref
  495.4 11.3 %shampoo.6 = (f32[176,2048]{1,0:T(8,128)}, f32[176,2048]{1,0:T(8,128)}, f32[192,64,64]{2,1,0:T(8,128)}, f32[192,128,128]{2,1,0:T(8,128)}) custom-call(bf16[176,2048]{1,0:T(8,128)(2,1)S(1)} %copy-done.11, f32[176,2048]{1,0:T(8,128)S(1)} %copy-done.5, bf16[192,64,64]{2,1,0:T(8,128)(2,1)S(1)} %copy.227.lr_ref, f32[192,128,128]{2,1,0:T(8,128)} %rr_ref.11, ...), custom_call_target="tpu_custom_call" | custom-call | flops 369098752 | bytes 15138816 | tf_op jit(solution)/shard_map/shampoo/pallas_call | solution.py:323
  544.9 17.9 %reduce-scatter.7.cloned.1.call-done = bf16[512,1408]{1,0:T(8,128)(2,1)} async-done(((bf16[2048,1408]{1,0:T(8,128)(2,1)}), bf16[512,1408]{1,0:T(8,128)(2,1)}) %reduce-scatter.7.cloned.1.call-update) | async-done | bytes 1441808 | tf_op jit(solution)/shard_map/reduce_scatter | solution.py:206
  585.7 8.6 %collective-permute-done.39 = bf16[128,1536]{1,0:T(8,128)(2,1)S(1)} collective-permute-done((bf16[128,1536]{1,0:T(8,128)(2,1)S(1)}, bf16[128,1536]{1,0:T(8,128)(2,1)S(1)}, u32[]{:S(2)}, u32[]{:S(2)}) %collective-permute-start.39) | collective-permute-done | bytes 393248 | tf_op jit(solution)/shard_map/ppermute | solution.py:100
  605.2 20.7 %collective-permute-done.41 = bf16[64,1536]{1,0:T(8,128)(2,1)S(1)} collective-permute-done((bf16[64,1536]{1,0:T(8,128)(2,1)S(1)}, bf16[64,1536]{1,0:T(8,128)(2,1)S(1)}, u32[]{:S(2)}, u32[]{:S(2)}) %collective-permute-start.41) | collective-permute-done | bytes 196640 | tf_op jit(solution)/shard_map/ppermute | solution.py:100
  629.0 13.4 %shampoo.7 = (f32[64,11264]{1,0:T(8,128)}, f32[64,11264]{1,0:T(8,128)}, f32[192,64,64]{2,1,0:T(8,128)}, f32[192,128,128]{2,1,0:T(8,128)}) custom-call(bf16[8,64,1408]{2,1,0:T(8,128)(2,1)} %all-to-all-done.2.g_ref, f32[64,11264]{1,0:T(8,128)S(1)} %copy-done.3, bf16[192,64,64]{2,1,0:T(8,128)(2,1)} %copy-done, ...), custom_call_target="tpu_custom_call", output_to_operand_aliasing={{2}: (6, {}), {3}: (7, {})} | custom-call | flops 738197504 | bytes 30277632 | tf_op jit(solution)/shard_map/shampoo/pallas_call | solution.py:323
  698.5 6.4 shampoo.8
  751.9 6.9 copy.243
  (730 shorter events, 433.3 us)
Async XLA Ops:
  52.4 23.3 %all-to-all-start.1 = ((bf16[8,64,1408]{2,1,0:T(8,128)(2,1)}), bf16[8,64,1408]{2,1,0:T(8,128)(2,1)S(1)}, u32[]{:S(2)}, u32[]{:S(2)}) async-start(bf16[8,64,1408]{2,1,0:T(8,128)(2,1)} %copy.212), calls=%async_computation.1 | async-start | bytes 2883584 | tf_op jit(solution)/shard_map/all_to_all | solution.py:195
  56.2 65.8 %all-gather.5.cloned.1.call-start = ((), (), s32[]{:S(2)}) async-start(), calls=%async_computation.9 | async-start | bytes 3932160 | tf_op jit(solution)/shard_map/all_gather | solution.py:190
  57.9 124.8 %all-gather.7.cloned.1.call-start = ((), (), s32[]{:S(2)}) async-start(), calls=%async_computation.10 | async-start | bytes 3604480 | tf_op jit(solution)/shard_map/all_gather | solution.py:190
  98.1 26.6 %collective-permute-start.3 = (bf16[512,1536]{1,0:T(8,128)(2,1)}, bf16[512,1536]{1,0:T(8,128)(2,1)}, u32[]{:S(2)}, u32[]{:S(2)}) collective-permute-start(bf16[512,1536]{1,0:T(8,128)(2,1)} %convolution_convert_fusion.5), channel_id=1, source_target_pairs={{0,4},{4,0},{8,12},{12,8},{16,20},{20,16},{24,28},{28,24},{1,5},{5... | collective-permute-start | bytes 4718600 | tf_op jit(solution)/shard_map/ppermute | solution.py:100
  124.7 144.8 %all-gather.9.cloned.1.call-start = ((), (), s32[]{:S(2)}) async-start(), calls=%async_computation.11 | async-start | bytes 3604480 | tf_op jit(solution)/shard_map/all_gather | solution.py:190
  212.1 118.3 %all-gather.11.cloned.1.call-start = ((), (), s32[]{:S(2)}) async-start(), calls=%async_computation.12 | async-start | bytes 3604480 | tf_op jit(solution)/shard_map/all_gather | solution.py:190
  232.2 40.7 %collective-permute-start.13 = (bf16[512,2048]{1,0:T(8,128)(2,1)}, bf16[512,2048]{1,0:T(8,128)(2,1)}, u32[]{:S(2)}, u32[]{:S(2)}) collective-permute-start(bf16[512,2048]{1,0:T(8,128)(2,1)} %convolution_convert_fusion.4), channel_id=1, source_target_pairs={{0,4},{4,0},{8,12},{12,8},{16,20},{20,16},{24,28},{28,24},{1,5},{5... | collective-permute-start | bytes 6291464 | tf_op jit(solution)/shard_map/ppermute | solution.py:100
  244.3 37.6 %collective-permute-start.26 = (bf16[128,2048]{1,0:T(8,128)(2,1)}, bf16[128,2048]{1,0:T(8,128)(2,1)}, u32[]{:S(2)}, u32[]{:S(2)}) collective-permute-start(bf16[128,2048]{1,0:T(8,128)(2,1)} %pad_maximum_fusion.16), channel_id=1, source_target_pairs={{0,16},{4,20},{8,24},{12,28},{16,0},{20,4},{24,8},{28,12},{1,17},{... | collective-permute-start | bytes 1572872 | tf_op jit(solution)/shard_map/ppermute | solution.py:100
  272.4 185.1 %reduce-scatter.5.cloned.1.call-start = ((), (), s32[]{:S(2)}) async-start(), calls=%async_computation.13 | async-start | bytes 3604480 | tf_op jit(solution)/shard_map/reduce_scatter | solution.py:206
  276.8 14.9 %collective-permute-start.14 = (bf16[128,2048]{1,0:T(8,128)(2,1)S(1)}, bf16[128,2048]{1,0:T(8,128)(2,1)S(1)}, u32[]{:S(2)}, u32[]{:S(2)}) collective-permute-start(bf16[128,2048]{1,0:T(8,128)(2,1)S(1)} %get-tuple-element.225), channel_id=1, source_target_pairs={{0,8},{4,12},{8,0},{12,4},{16,24},{20,28},{24,16},{28,20},{1,9},{5... | collective-permute-start | bytes 1572872 | tf_op jit(solution)/shard_map/ppermute | solution.py:100
  280.6 22.3 %collective-permute-start.25 = (bf16[128,2048]{1,0:T(8,128)(2,1)S(1)}, bf16[128,2048]{1,0:T(8,128)(2,1)S(1)}, u32[]{:S(2)}, u32[]{:S(2)}) collective-permute-start(bf16[128,2048]{1,0:T(8,128)(2,1)S(1)} %pad_maximum_fusion.15), channel_id=1, source_target_pairs={{0,8},{4,12},{8,0},{12,4},{16,24},{20,28},{24,16},{28,20},{1,9},{5... | collective-permute-start | bytes 1572872 | tf_op jit(solution)/shard_map/ppermute | solution.py:100
  397.3 14.6 %collective-permute-start.28 = (bf16[512,2048]{1,0:T(8,128)(2,1)}, bf16[512,2048]{1,0:T(8,128)(2,1)}, u32[]{:S(2)}, u32[]{:S(2)}) collective-permute-start(bf16[512,2048]{1,0:T(8,128)(2,1)} %add_convert_fusion), channel_id=1, source_target_pairs={{0,4},{4,0},{8,12},{12,8},{16,20},{20,16},{24,28},{28,24},{1,5},{5... | collective-permute-start | bytes 6291464 | tf_op jit(solution)/shard_map/ppermute | solution.py:100
  397.4 165.4 %reduce-scatter.7.cloned.1.call-start = ((), (), s32[]{:S(2)}) async-start(), calls=%async_computation.14 | async-start | bytes 7208960 | tf_op jit(solution)/shard_map/reduce_scatter | solution.py:206
  462.4 184.9 %reduce-scatter.9.cloned.1.call-start = ((), (), s32[]{:S(2)}) async-start(), calls=%async_computation.15 | async-start | bytes 3932160 | tf_op jit(solution)/shard_map/reduce_scatter | solution.py:206
  480.0 28.8 %collective-permute-start.37 = (bf16[512,2048]{1,0:T(8,128)(2,1)}, bf16[512,2048]{1,0:T(8,128)(2,1)}, u32[]{:S(2)}, u32[]{:S(2)}) collective-permute-start(bf16[512,2048]{1,0:T(8,128)(2,1)} %get-tuple-element.253), channel_id=1, source_target_pairs={{0,4},{4,0},{8,12},{12,8},{16,20},{20,16},{24,28},{28,24},{1,5},{5... | collective-permute-start | bytes 6291464 | tf_op jit(solution)/shard_map/ppermute | solution.py:100
  598.5 30.5 %all-to-all-start.2 = ((bf16[8,64,1408]{2,1,0:T(8,128)(2,1)}), bf16[8,64,1408]{2,1,0:T(8,128)(2,1)}, u32[]{:S(2)}, u32[]{:S(2)}) async-start(bf16[8,64,1408]{2,1,0:T(8,128)(2,1)} %bitcast.252), calls=%async_computation.5 | async-start | bytes 2883584 | tf_op jit(solution)/shard_map/all_to_all | solution.py:195
  603.1 22.7 %collective-permute-start.41 = (bf16[64,1536]{1,0:T(8,128)(2,1)S(1)}, bf16[64,1536]{1,0:T(8,128)(2,1)S(1)}, u32[]{:S(2)}, u32[]{:S(2)}) collective-permute-start(bf16[64,1536]{1,0:T(8,128)(2,1)S(1)} %slice.1186), channel_id=1, source_target_pairs={{0,16},{4,20},{8,24},{12,28},{16,0},{20,4},{24,8},{28,12},{1,17},{... | collective-permute-start | bytes 589832 | tf_op jit(solution)/shard_map/ppermute | solution.py:100
  627.2 17.0 %collective-permute-start.44 = (bf16[64,1536]{1,0:T(8,128)(2,1)}, bf16[64,1536]{1,0:T(8,128)(2,1)S(1)}, u32[]{:S(2)}, u32[]{:S(2)}) collective-permute-start(bf16[64,1536]{1,0:T(8,128)(2,1)} %get-tuple-element.295), channel_id=1, source_target_pairs={{0,8},{4,12},{8,0},{12,4},{16,24},{20,28},{24,16},{28,20},{1,9},{5... | collective-permute-start | bytes 589832 | tf_op jit(solution)/shard_map/ppermute | solution.py:100
  628.7 16.7 %collective-permute-start.43 = (bf16[64,1536]{1,0:T(8,128)(2,1)}, bf16[64,1536]{1,0:T(8,128)(2,1)}, u32[]{:S(2)}, u32[]{:S(2)}) collective-permute-start(bf16[64,1536]{1,0:T(8,128)(2,1)} %get-tuple-element.297), channel_id=1, source_target_pairs={{0,16},{4,20},{8,24},{12,28},{16,0},{20,4},{24,8},{28,12},{1,17},{... | collective-permute-start | bytes 589832 | tf_op jit(solution)/shard_map/ppermute | solution.py:100
  683.2 30.1 %collective-permute-start.48 = (bf16[512,2048]{1,0:T(8,128)(2,1)}, bf16[512,2048]{1,0:T(8,128)(2,1)}, u32[]{:S(2)}, u32[]{:S(2)}) collective-permute-start(bf16[512,2048]{1,0:T(8,128)(2,1)} %convolution_convert_fusion.3), channel_id=1, source_target_pairs={{0,4},{4,0},{8,12},{12,8},{16,20},{20,16},{24,28},{28,24},{1,5},{5... | collective-permute-start | bytes 6291464 | tf_op jit(solution)/shard_map/ppermute | solution.py:100
  690.5 19.8 %collective-permute-start.54 = (bf16[256,512]{1,0:T(8,128)(2,1)}, bf16[256,512]{1,0:T(8,128)(2,1)}, u32[]{:S(2)}, u32[]{:S(2)}) collective-permute-start(bf16[256,512]{1,0:T(8,128)(2,1)} %fusion.124), channel_id=1, source_target_pairs={{0,8},{4,12},{8,0},{12,4},{16,24},{20,28},{24,16},{28,20},{1,9},{5... | collective-permute-start | bytes 786440 | tf_op jit(solution)/shard_map/ppermute | solution.py:100
  696.1 48.7 %reduce-scatter.11.cloned.1.call-start = ((), (), s32[]{:S(2)}) async-start(), calls=%async_computation.16 | async-start | bytes 983040 | tf_op jit(solution)/shard_map/reduce_scatter | solution.py:206
  723.5 20.6 %all-to-all-start.4 = ((f32[32,1,256]{2,1,0:T(1,128)}), f32[32,1,256]{2,1,0:T(1,128)S(1)}, u32[]{:S(2)}, u32[]{:S(2)}) async-start(f32[32,1,256]{2,1,0:T(1,128)} %all_to_all.22), calls=%async_computation.8 | async-start | bytes 65536 | tf_op jit(solution)/shard_map/all_to_all | solution.py:560
  742.6 16.9 %collective-permute-start.52 = (bf16[64,2048]{1,0:T(8,128)(2,1)}, bf16[64,2048]{1,0:T(8,128)(2,1)}, u32[]{:S(2)}, u32[]{:S(2)}) collective-permute-start(bf16[64,2048]{1,0:T(8,128)(2,1)} %slice.1179), channel_id=1, source_target_pairs={{0,8},{4,12},{8,0},{12,4},{16,24},{20,28},{24,16},{28,20},{1,9},{5... | collective-permute-start | bytes 786440 | tf_op jit(solution)/shard_map/ppermute | solution.py:100
  (198 other events, 2389.3 us)
Sparse Core Ops, SparseCore 0:
  59.1 62.7 all-gather.4
  124.8 57.8 all-gather.6
  212.2 57.2 all-gather.8
  272.5 57.8 all-gather.10
  397.5 55.1 reduce-scatter.4
  462.5 100.2 reduce-scatter.6
  576.9 60.8 reduce-scatter.8
  705.0 24.2 reduce-scatter.10

commit v3 on v2

--- a/solution.py
+++ b/solution.py
@@ -400,7 +400,7 @@
     query_out = jnp.concatenate([query_parts.reshape(-1, D), master_out.astype(bf16)], axis=0)
     query_out = lay.gather_shard(after(query_out, weight_small))
     weight_out = query_out[:, -out_rows:].reshape(-1, D)
-    split = gate_up_parts.shape[1] // 2
+    split = gate_up_parts.shape[1] * 3 // 4
     gate_up_first = lay.gather_shard(after(gate_up_parts[:, :split], query_out))
     gate_up_second = lay.gather_shard(after(gate_up_parts[:, split:], gate_up_first))
     weight_gu = whole_shard(jnp.concatenate([gate_up_first, gate_up_second], axis=2))
@@ -450,11 +450,11 @@
     own_low = jnp.concatenate(
         [rms_norm(latent, gain_query), own_keys, latent_kv[:, QR + HD :]], axis=1
     )
-    all_low = lay.gather(own_low.astype(bf16), (gate_up_first,))
+    all_low = lay.gather(own_low.astype(bf16))
     latent_norm = all_low[:, :QR]
     keys_all = all_low[:, QR : QR + HD]
     values_all = all_low[:, QR + HD :]
-    query_lin = dot(latent_norm, weight_qb)
+    query_lin = after(dot(latent_norm, weight_qb), gate_up_first)
     queries = [
         rotate(query_lin[:, h * HD : (h + 1) * HD], cosine_table, sine_table).astype(bf16)
         for h in range(heads_here)
@@ -560,7 +560,7 @@
     gain_grad = lax.all_to_all(gain_grad, ("seq", "row"), 0, 0, tiled=True)
     gain_grad = jnp.sum(gain_grad, axis=0)[:gains_here]
 
-    output = middle + lay.scatter_dots([(after(hidden, part_small), weight_down, dot)])
+    output = middle + lay.scatter_dots([(after(hidden, sums), weight_down, dot)])
     sum_small = lay.sum_shard(part_small)
     sum_qb = sum_qb_out[:-out_rows].reshape(GROUP, -1, HQ * HD // GROUP)
     parts_qb = lay.exchange(after(sum_qb, part_small))

time: 786 us -> 782 us (level)
  waiting for transfers between devices: 274 us -> 258 us
  other arithmetic: 77.3 us -> 88.5 us
    ppermute x56, waiting for transfers between devices: 155 us -> 137 us  [swap(): return lax.ppermute(values, 'seq', [(s, s ^ stride) for s in range(self.n)])]
    all_to_all x4, waiting for transfers between devices: 20.8 us -> 4.75 us  [exchange(): return lax.all_to_all(values, 'seq', 0, 0, axis_index_groups=groups)]
    all_gather x4, waiting for transfers between devices: 80.4 us -> 92.4 us  [gather_shard(): flat = lax.all_gather(flat, 'row', axis=0, tiled=True)]
    unnamed x327 -> x293, local copies, waits for them, and re-layouts: 56.1 us -> 46.9 us
    slice x47 -> x48, local copies, waits for them, and re-layouts: 37.5 us -> 36.5 us  [after(): entry = other[(0,) * other.ndim].astype(f32) * 0.0]
  transfers between devices with their start and end apart: 69 -> 69, of which waited for: 38 -> 41; matrix products, arithmetic and copies ran while one was open for 26% -> 30% of each run, Pallas kernels for 5% -> 5%
where the time goes in v3:
time: 782 us; the launch traced here: 771 us
  waiting for transfers between devices  258 us (33%)
  local copies, waits for them, and re-layouts  124 us (16%)
  matrix products  107 us (14%)
  other arithmetic  88.5 us (11%)
  starting transfers between devices  79.8 us (10%)
  between operations  48.9 us (6%)
  Pallas kernels  41.2 us (5%)
  blocking collectives  22.7 us (3%)
    ppermute x56, waiting for transfers between devices, swap(): return lax.ppermute(values, 'seq', [(s, s ^ stride) for s in range(self.n)])  137 us
    all_gather x4, waiting for transfers between devices, gather_shard(): flat = lax.all_gather(flat, 'row', axis=0, tiled=True)  92.4 us
    ppermute x56, starting transfers between devices, swap(): return lax.ppermute(values, 'seq', [(s, s ^ stride) for s in range(self.n)])  58.3 us
    unnamed x293, local copies, waits for them, and re-layouts  46.9 us
    pallas_call x6, Pallas kernels, shampoo(): pl.pallas_call(functools.partial(shampoo_kernel, count, segments), grid=(...  41.2 us
    dot_general x11, matrix products, dot_nt(): lax.dot_general(left, right, (((1,), (1,)), ((), ())), preferred_element_...  40.7 us
    dot_general x12, matrix products, dot(): lax.dot_general(left, right, (((1,), (0,)), ((), ())), preferred_element_...  37.5 us
    slice x48, local copies, waits for them, and re-layouts, after(): entry = other[(0,) * other.ndim].astype(f32) * 0.0  36.5 us
  transfers between devices with their start and end apart: 69, of which 41 were waited for; matrix products, arithmetic and copies ran while one was open for 30% of the time, Pallas kernels for 5%

profile of v3, /device:TPU:0, one launch (start us, length us, event | category | flops | bytes accessed | tf_op | source)
XLA Modules:
  0.0 770.6 jit_solution(18226990557222573570)
XLA Ops:
  31.2 22.7 %all_gather.15 = bf16[320,1536]{1,0:T(8,128)(2,1)} all-gather(bf16[80,1536]{1,0:T(8,128)(2,1)S(1)} %fusion.135), channel_id=1, replica_groups=mesh['seq'=8,'row'=4] {'row'}, dimensions={0}, use_global_device_ids=true | all-gather | bytes 1228800 | tf_op jit(solution)/shard_map/all_gather | solution.py:190
  86.1 38.0 %all-gather.5.cloned.1.call-done = bf16[768,2048]{1,0:T(8,128)(2,1)} async-done(((bf16[192,2048]{1,0:T(8,128)(2,1)}), bf16[768,2048]{1,0:T(8,128)(2,1)}) %all-gather.5.cloned.1.call-update) | async-done | bytes 3145744 | tf_op jit(solution)/shard_map/all_gather | solution.py:190
  133.1 6.0 collective-permute-done.4
  190.4 46.3 %all-gather.7.cloned.1.call-done = bf16[1536,1408]{1,0:T(8,128)(2,1)} async-done(((bf16[384,1408]{1,0:T(8,128)(2,1)}), bf16[1536,1408]{1,0:T(8,128)(2,1)}) %all-gather.7.cloned.1.call-update) | async-done | bytes 4325392 | tf_op jit(solution)/shard_map/all_gather | solution.py:190
  290.3 6.2 collective-permute-done.14
  301.6 6.2 collective-permute-done.25
  326.4 8.1 %all-gather.11.cloned.1.call-done = bf16[704,2048]{1,0:T(8,128)(2,1)} async-done(((bf16[176,2048]{1,0:T(8,128)(2,1)}), bf16[704,2048]{1,0:T(8,128)(2,1)}) %all-gather.11.cloned.1.call-update) | async-done | bytes 2883600 | tf_op jit(solution)/shard_map/all_gather | solution.py:190
  367.7 9.6 %fusion.184 = f32[1024,1408]{1,0:T(8,128)S(1)} fusion(bf16[1024,2048]{1,0:T(8,128)(2,1)} %constant_dynamic-update-slice_fusion.13, bf16[2048,1408]{1,0:T(8,128)(2,1)S(1)} %bitcast.229), kind=kOutput, calls=%fused_computation.446 | convolution fusion | flops 5905580032 | bytes 15728640 | tf_op jit(solution)/shard_map/dot_general | solution.py:59
  377.3 7.7 %multiply_convert_fusion.2 = (bf16[1024,704]{1,0:T(8,128)(2,1)S(1)}, bf16[1024,704]{1,0:T(8,128)(2,1)}, bf16[1024,704]{1,0:T(8,128)(2,1)S(1)}) fusion(f32[1024,1408]{1,0:T(8,128)S(1)} %fusion.184, bf16[1024,2048]{1,0:T(8,128)(2,1)} %constant_dynamic-update-slice_fusion.22, bf16[704,2048]{1,0:T(8,128)(2,1)S(1)} %copy-done.42), kind=kOutput, calls=%fused_computation.34 | convolution fusion | flops 2964324352 | bytes 17170432 | tf_op jit(solution)/shard_map/dot_general | solution.py:63
  386.1 7.0 convolution_convert_fusion.1
  394.9 7.7 add_convert_fusion
  402.7 9.4 %convolution_convert_fusion = bf16[2048,1408]{1,0:T(8,128)(2,1)S(1)} fusion(bf16[1024,2048]{1,0:T(8,128)(2,1)} %constant_dynamic-update-slice_fusion.13, bf16[1024,704]{1,0:T(8,128)(2,1)S(1)} %get-tuple-element.204, bf16[1024,704]{1,0:T(8,128)(2,1)} %get-tuple-element.205), kind=kOutput, calls=%fused_computation | convolution fusion | flops 5914230784 | bytes 12845056 | tf_op jit(solution)/shard_map/dot_general | solution.py:67
  416.8 7.0 fusion.182
  427.0 11.4 %collective-permute-done.29 = bf16[128,2048]{1,0:T(8,128)(2,1)S(1)} collective-permute-done((bf16[128,2048]{1,0:T(8,128)(2,1)S(1)}, bf16[128,2048]{1,0:T(8,128)(2,1)S(1)}, u32[]{:S(2)}, u32[]{:S(2)}) %collective-permute-start.29) | collective-permute-done | bytes 524320 | tf_op jit(solution)/shard_map/ppermute | solution.py:100
  467.1 8.6 %collective-permute-done.36 = bf16[128,2048]{1,0:T(8,128)(2,1)S(1)} collective-permute-done((bf16[128,2048]{1,0:T(8,128)(2,1)S(1)}, bf16[128,2048]{1,0:T(8,128)(2,1)S(1)}, u32[]{:S(2)}, u32[]{:S(2)}) %collective-permute-start.36) | collective-permute-done | bytes 524320 | tf_op jit(solution)/shard_map/ppermute | solution.py:100
  484.6 5.6 copy.209.lr_ref
  490.3 7.6 copy.210.ls_ref
  500.4 11.3 %shampoo.6 = (f32[176,2048]{1,0:T(8,128)}, f32[176,2048]{1,0:T(8,128)}, f32[192,64,64]{2,1,0:T(8,128)}, f32[192,128,128]{2,1,0:T(8,128)}) custom-call(bf16[176,2048]{1,0:T(8,128)(2,1)S(1)} %copy-done.11, f32[176,2048]{1,0:T(8,128)S(1)} %copy-done.5, bf16[192,64,64]{2,1,0:T(8,128)(2,1)S(1)} %copy.209.lr_ref, f32[192,128,128]{2,1,0:T(8,128)} %rr_ref.11, ...), custom_call_target="tpu_custom_call" | custom-call | flops 369098752 | bytes 15138816 | tf_op jit(solution)/shard_map/shampoo/pallas_call | solution.py:323
  546.6 21.0 %reduce-scatter.7.cloned.1.call-done = bf16[512,1408]{1,0:T(8,128)(2,1)} async-done(((bf16[2048,1408]{1,0:T(8,128)(2,1)}), bf16[512,1408]{1,0:T(8,128)(2,1)}) %reduce-scatter.7.cloned.1.call-update) | async-done | bytes 1441808 | tf_op jit(solution)/shard_map/reduce_scatter | solution.py:206
  596.1 21.5 %collective-permute-done.40 = bf16[128,1536]{1,0:T(8,128)(2,1)S(1)} collective-permute-done((bf16[128,1536]{1,0:T(8,128)(2,1)S(1)}, bf16[128,1536]{1,0:T(8,128)(2,1)S(1)}, u32[]{:S(2)}, u32[]{:S(2)}) %collective-permute-start.40) | collective-permute-done | bytes 393248 | tf_op jit(solution)/shard_map/ppermute | solution.py:100
  622.5 13.7 %shampoo.7 = (f32[64,11264]{1,0:T(8,128)}, f32[64,11264]{1,0:T(8,128)}, f32[192,64,64]{2,1,0:T(8,128)}, f32[192,128,128]{2,1,0:T(8,128)}) custom-call(bf16[8,64,1408]{2,1,0:T(8,128)(2,1)} %all-to-all-done.2.g_ref, f32[64,11264]{1,0:T(8,128)S(1)} %copy-done.3, bf16[192,64,64]{2,1,0:T(8,128)(2,1)} %copy-done, ...), custom_call_target="tpu_custom_call", output_to_operand_aliasing={{2}: (6, {}), {3}: (7, {})} | custom-call | flops 738197504 | bytes 30277632 | tf_op jit(solution)/shard_map/shampoo/pallas_call | solution.py:323
  676.9 8.1 %collective-permute-done.43 = bf16[128,2048]{1,0:T(8,128)(2,1)S(1)} collective-permute-done((bf16[128,2048]{1,0:T(8,128)(2,1)S(1)}, bf16[128,2048]{1,0:T(8,128)(2,1)S(1)}, u32[]{:S(2)}, u32[]{:S(2)}) %collective-permute-start.43) | collective-permute-done | bytes 524320 | tf_op jit(solution)/shard_map/ppermute | solution.py:100
  694.4 6.5 shampoo.8
  756.7 6.7 copy.226
  (697 shorter events, 417.9 us)
Async XLA Ops:
  27.5 33.8 %all-to-all-start.1 = ((bf16[8,64,1408]{2,1,0:T(8,128)(2,1)}), bf16[8,64,1408]{2,1,0:T(8,128)(2,1)S(1)}, u32[]{:S(2)}, u32[]{:S(2)}) async-start(bf16[8,64,1408]{2,1,0:T(8,128)(2,1)} %copy.198), calls=%async_computation.1 | async-start | bytes 2883584 | tf_op jit(solution)/shard_map/all_to_all | solution.py:195
  31.1 93.0 %all-gather.5.cloned.1.call-start = ((), (), s32[]{:S(2)}) async-start(), calls=%async_computation.9 | async-start | bytes 3932160 | tf_op jit(solution)/shard_map/all_gather | solution.py:190
  60.1 176.6 %all-gather.7.cloned.1.call-start = ((), (), s32[]{:S(2)}) async-start(), calls=%async_computation.10 | async-start | bytes 5406720 | tf_op jit(solution)/shard_map/all_gather | solution.py:190
  84.0 42.0 %collective-permute-start.3 = (bf16[512,1536]{1,0:T(8,128)(2,1)}, bf16[512,1536]{1,0:T(8,128)(2,1)}, u32[]{:S(2)}, u32[]{:S(2)}) collective-permute-start(bf16[512,1536]{1,0:T(8,128)(2,1)} %convolution_convert_fusion.5), channel_id=1, source_target_pairs={{0,4},{4,0},{8,12},{12,8},{16,20},{20,16},{24,28},{28,24},{1,5},{5... | collective-permute-start | bytes 4718600 | tf_op jit(solution)/shard_map/ppermute | solution.py:100
  156.3 118.5 %all-gather.9.cloned.1.call-start = ((), (), s32[]{:S(2)}) async-start(), calls=%async_computation.11 | async-start | bytes 1802240 | tf_op jit(solution)/shard_map/all_gather | solution.py:190
  239.3 95.2 %all-gather.11.cloned.1.call-start = ((), (), s32[]{:S(2)}) async-start(), calls=%async_computation.12 | async-start | bytes 3604480 | tf_op jit(solution)/shard_map/all_gather | solution.py:190
  261.3 16.4 %collective-permute-start.13 = (bf16[512,2048]{1,0:T(8,128)(2,1)}, bf16[512,2048]{1,0:T(8,128)(2,1)}, u32[]{:S(2)}, u32[]{:S(2)}) collective-permute-start(bf16[512,2048]{1,0:T(8,128)(2,1)} %convolution_convert_fusion.4), channel_id=1, source_target_pairs={{0,4},{4,0},{8,12},{12,8},{16,20},{20,16},{24,28},{28,24},{1,5},{5... | collective-permute-start | bytes 6291464 | tf_op jit(solution)/shard_map/ppermute | solution.py:100
  273.4 15.1 %collective-permute-start.26 = (bf16[128,2048]{1,0:T(8,128)(2,1)}, bf16[128,2048]{1,0:T(8,128)(2,1)}, u32[]{:S(2)}, u32[]{:S(2)}) collective-permute-start(bf16[128,2048]{1,0:T(8,128)(2,1)} %pad_maximum_fusion.16), channel_id=1, source_target_pairs={{0,16},{4,20},{8,24},{12,28},{16,0},{20,4},{24,8},{28,12},{1,17},{... | collective-permute-start | bytes 1572872 | tf_op jit(solution)/shard_map/ppermute | solution.py:100
  277.6 184.5 %reduce-scatter.5.cloned.1.call-start = ((), (), s32[]{:S(2)}) async-start(), calls=%async_computation.13 | async-start | bytes 3604480 | tf_op jit(solution)/shard_map/reduce_scatter | solution.py:206
  281.6 14.9 %collective-permute-start.14 = (bf16[128,2048]{1,0:T(8,128)(2,1)S(1)}, bf16[128,2048]{1,0:T(8,128)(2,1)S(1)}, u32[]{:S(2)}, u32[]{:S(2)}) collective-permute-start(bf16[128,2048]{1,0:T(8,128)(2,1)S(1)} %get-tuple-element.225), channel_id=1, source_target_pairs={{0,8},{4,12},{8,0},{12,4},{16,24},{20,28},{24,16},{28,20},{1,9},{5... | collective-permute-start | bytes 1572872 | tf_op jit(solution)/shard_map/ppermute | solution.py:100
  283.1 15.3 %collective-permute-start.15 = (bf16[128,2048]{1,0:T(8,128)(2,1)S(1)}, bf16[128,2048]{1,0:T(8,128)(2,1)S(1)}, u32[]{:S(2)}, u32[]{:S(2)}) collective-permute-start(bf16[128,2048]{1,0:T(8,128)(2,1)S(1)} %get-tuple-element.226), channel_id=1, source_target_pairs={{0,16},{4,20},{8,24},{12,28},{16,0},{20,4},{24,8},{28,12},{1,17},{... | collective-permute-start | bytes 1572872 | tf_op jit(solution)/shard_map/ppermute | solution.py:100
  284.5 23.3 %collective-permute-start.25 = (bf16[128,2048]{1,0:T(8,128)(2,1)S(1)}, bf16[128,2048]{1,0:T(8,128)(2,1)S(1)}, u32[]{:S(2)}, u32[]{:S(2)}) collective-permute-start(bf16[128,2048]{1,0:T(8,128)(2,1)S(1)} %pad_maximum_fusion.15), channel_id=1, source_target_pairs={{0,8},{4,12},{8,0},{12,4},{16,24},{20,28},{24,16},{28,20},{1,9},{5... | collective-permute-start | bytes 1572872 | tf_op jit(solution)/shard_map/ppermute | solution.py:100
  402.6 165.0 %reduce-scatter.7.cloned.1.call-start = ((), (), s32[]{:S(2)}) async-start(), calls=%async_computation.14 | async-start | bytes 7208960 | tf_op jit(solution)/shard_map/reduce_scatter | solution.py:206
  424.0 14.4 %collective-permute-start.29 = (bf16[128,2048]{1,0:T(8,128)(2,1)S(1)}, bf16[128,2048]{1,0:T(8,128)(2,1)S(1)}, u32[]{:S(2)}, u32[]{:S(2)}) collective-permute-start(bf16[128,2048]{1,0:T(8,128)(2,1)S(1)} %get-tuple-element.223), channel_id=1, source_target_pairs={{0,8},{4,12},{8,0},{12,4},{16,24},{20,28},{24,16},{28,20},{1,9},{5... | collective-permute-start | bytes 1572872 | tf_op jit(solution)/shard_map/ppermute | solution.py:100
  467.1 187.4 %reduce-scatter.9.cloned.1.call-start = ((), (), s32[]{:S(2)}) async-start(), calls=%async_computation.15 | async-start | bytes 3932160 | tf_op jit(solution)/shard_map/reduce_scatter | solution.py:206
  484.6 29.2 %collective-permute-start.37 = (bf16[512,2048]{1,0:T(8,128)(2,1)}, bf16[512,2048]{1,0:T(8,128)(2,1)}, u32[]{:S(2)}, u32[]{:S(2)}) collective-permute-start(bf16[512,2048]{1,0:T(8,128)(2,1)} %get-tuple-element.253), channel_id=1, source_target_pairs={{0,4},{4,0},{8,12},{12,8},{16,20},{20,16},{24,28},{28,24},{1,5},{5... | collective-permute-start | bytes 6291464 | tf_op jit(solution)/shard_map/ppermute | solution.py:100
  572.5 18.1 %collective-permute-start.38 = (bf16[512,1536]{1,0:T(8,128)(2,1)}, bf16[512,1536]{1,0:T(8,128)(2,1)}, u32[]{:S(2)}, u32[]{:S(2)}) collective-permute-start(bf16[512,1536]{1,0:T(8,128)(2,1)} %fusion.4), channel_id=1, source_target_pairs={{0,4},{4,0},{8,12},{12,8},{16,20},{20,16},{24,28},{28,24},{1,5},{5... | collective-permute-start | bytes 4718600 | tf_op jit(solution)/shard_map/ppermute | solution.py:100
  586.1 36.3 %all-to-all-start.2 = ((bf16[8,64,1408]{2,1,0:T(8,128)(2,1)}), bf16[8,64,1408]{2,1,0:T(8,128)(2,1)}, u32[]{:S(2)}, u32[]{:S(2)}) async-start(bf16[8,64,1408]{2,1,0:T(8,128)(2,1)} %bitcast.250), calls=%async_computation.5 | async-start | bytes 2883584 | tf_op jit(solution)/shard_map/all_to_all | solution.py:195
  590.6 159.0 %reduce-scatter.11.cloned.1.call-start = ((), (), s32[]{:S(2)}) async-start(), calls=%async_computation.16 | async-start | bytes 983040 | tf_op jit(solution)/shard_map/reduce_scatter | solution.py:206
  592.7 24.9 %collective-permute-start.40 = (bf16[128,1536]{1,0:T(8,128)(2,1)S(1)}, bf16[128,1536]{1,0:T(8,128)(2,1)S(1)}, u32[]{:S(2)}, u32[]{:S(2)}) collective-permute-start(bf16[128,1536]{1,0:T(8,128)(2,1)S(1)} %get-tuple-element.229), channel_id=1, source_target_pairs={{0,16},{4,20},{8,24},{12,28},{16,0},{20,4},{24,8},{28,12},{1,17},{... | collective-permute-start | bytes 1179656 | tf_op jit(solution)/shard_map/ppermute | solution.py:100
  594.6 24.1 %collective-permute-start.39 = (bf16[128,1536]{1,0:T(8,128)(2,1)S(1)}, bf16[128,1536]{1,0:T(8,128)(2,1)S(1)}, u32[]{:S(2)}, u32[]{:S(2)}) collective-permute-start(bf16[128,1536]{1,0:T(8,128)(2,1)S(1)} %get-tuple-element.230), channel_id=1, source_target_pairs={{0,8},{4,12},{8,0},{12,4},{16,24},{20,28},{24,16},{28,20},{1,9},{5... | collective-permute-start | bytes 1179656 | tf_op jit(solution)/shard_map/ppermute | solution.py:100
  621.9 17.8 %collective-permute-start.41 = (bf16[64,1536]{1,0:T(8,128)(2,1)S(1)}, bf16[64,1536]{1,0:T(8,128)(2,1)S(1)}, u32[]{:S(2)}, u32[]{:S(2)}) collective-permute-start(bf16[64,1536]{1,0:T(8,128)(2,1)S(1)} %slice.1191), channel_id=1, source_target_pairs={{0,16},{4,20},{8,24},{12,28},{16,0},{20,4},{24,8},{28,12},{1,17},{... | collective-permute-start | bytes 589832 | tf_op jit(solution)/shard_map/ppermute | solution.py:100
  676.9 29.1 %collective-permute-start.52 = (bf16[512,1536]{1,0:T(8,128)(2,1)}, bf16[512,1536]{1,0:T(8,128)(2,1)}, u32[]{:S(2)}, u32[]{:S(2)}) collective-permute-start(bf16[512,1536]{1,0:T(8,128)(2,1)} %get-tuple-element.291), channel_id=1, source_target_pairs={{0,4},{4,0},{8,12},{12,8},{16,20},{20,16},{24,28},{28,24},{1,5},{5... | collective-permute-start | bytes 4718600 | tf_op jit(solution)/shard_map/ppermute | solution.py:100
  702.8 24.4 %collective-permute-start.45 = (bf16[64,2048]{1,0:T(8,128)(2,1)}, bf16[64,2048]{1,0:T(8,128)(2,1)}, u32[]{:S(2)}, u32[]{:S(2)}) collective-permute-start(bf16[64,2048]{1,0:T(8,128)(2,1)} %slice.1185), channel_id=1, source_target_pairs={{0,16},{4,20},{8,24},{12,28},{16,0},{20,4},{24,8},{28,12},{1,17},{... | collective-permute-start | bytes 786440 | tf_op jit(solution)/shard_map/ppermute | solution.py:100
  (181 other events, 2115.7 us)
Sparse Core Ops, SparseCore 0:
  60.3 63.7 all-gather.4
  156.5 80.1 all-gather.6
  239.5 33.4 all-gather.8
  277.7 56.7 all-gather.10
  402.7 55.1 reduce-scatter.4
  467.2 100.3 reduce-scatter.6
  581.1 60.9 reduce-scatter.8
  712.6 23.1 reduce-scatter.10
